TPU v7x, 128 devices: a whole 4x4x4 slice. The times are simulated.
128 devices in a mesh: group: 2 (over z_lo), seq: 16 (over x, z_hi, core), dp: 4 (over y).
Axes of the slice: x: 4, y: 4, z: 4 (z_hi: 2, z_lo: 2; z = z_hi * 2 + z_lo), core: 2. Of those that a mesh axis runs over, the one named last changes fastest.
Arguments:
- latent_tokens: bfloat16 [8, 4096, 3072], P(('group', 'dp'), 'seq'), may hold values from -6 to 6
- modulation: float32 [8, 2, 3072], P(('group', 'dp')), may hold values from -3 to 3, as said below
- w_qkv: bfloat16 [3, 3072, 2048], P(None, None, 'seq'), may hold values from -0.108253175 to 0.108253175, as said below
- w_out: bfloat16 [2048, 64], replicated, may hold values from -0.125 to 0.125
- noisy_latents: bfloat16 [8, 16, 4, 32, 128], P(('group', 'dp'), None, None, 'seq'), may hold values from -6 to 6
- queue: int32 [8], replicated, may hold values from 0 to 7, each once
- frame_counts: int32 [8], replicated, may hold values from 1 to 4, 24 in all
- conv_w: bfloat16 [512, 432], replicated, may hold values from -0.3125 to 0.3125
- conv_b: float32 [512], replicated, may hold values from -1 to 1
Outputs:
- attended: bfloat16 [8, 4096, 2048], P(('group', 'dp'), 'seq')
- decoded: bfloat16 [8, 512, 4, 32, 128], P(('group', 'dp'), None, None, 'seq')
Inputs may be any that keep to these rules, and one draw needn't show every extreme that they name: `queue`: each request appears once. `frame_counts`: some request has all 4 frames. `modulation`: row 0 holds the shift, row 1 the scale. `w_qkv`: query, key and value blocks in that order.
All inputs are finite; a program needn't handle non-finite values.
Results may differ from a plain program's by a relative error of at most 0.012.
Values may be sent and summed in bfloat16 or wider, within the bound.
No kernel may reach another device: no remote copies, remote signals or barrier semaphores. Data moves between devices by JAX's collectives and lax.ppermute only.
A program may use at most 192 MiB of HBM per device.

v0:
```python
import functools
import math

import jax
import jax.numpy as jnp
from jax import lax
from jax.experimental import pallas as pl
from jax.experimental.pallas import tpu as pltpu
from jax.sharding import PartitionSpec as P

HEAD_DIM = 128
EVERY = ("group", "seq", "dp")
XS, ZS, YS = (4, 4, 4)
VMEM_BYTES = 12 << 20
QUERY_SCALE = math.log2(math.e) / math.sqrt(HEAD_DIM)
TINY = pl.CostEstimate(flops=1, bytes_accessed=1, transcendentals=0)
NT = (((1,), (1,)), ((), ()))


def linear(x, y, z, core):
    return ((z % 2) * 16 + (x * 2 + z // 2) * 2 + core) * YS + y


def moved(array, move):
    perm = []
    for x in range(XS):
        for y in range(YS):
            for z in range(ZS):
                for core in range(2):
                    to = move(x, y, z, core)
                    there = linear(to[0] % XS, to[1] % YS, to[2] % ZS, to[3])
                    perm.append((linear(x, y, z, core), there))
    return lax.ppermute(array, EVERY, perm)


def right(x, y, z, core):
    return (x + 1, y, z, core)


def left(x, y, z, core):
    return (x - 1, y, z, core)


def other_core(x, y, z, core):
    return (x, y, z, 1 - core)


def opposite_z(x, y, z, core):
    return (x, y, z + 2, core)


def mirrored_z(x, y, z, core):
    return (x, y, 3 - z, core)


def project_kernel(n_tokens, part_ref, *refs):
    tokens = refs[:n_tokens]
    w_ref = refs[n_tokens]
    w_parts = refs[n_tokens + 1 : n_tokens + 5]
    own_ref, away_ref = refs[n_tokens + 5 :]

    def step(c, carry):
        total = None
        for k in range(4):
            depth = w_parts[k].shape[1]
            at = pl.multiple_of(part_ref[k] * depth, depth)
            rows = jnp.concatenate([t[:, pl.ds(at, depth)] for t in tokens], axis=0)
            columns = jnp.concatenate([w_ref[c, pl.ds(at, depth), :], w_parts[k][c]], axis=1)
            term = jnp.dot(rows, columns, preferred_element_type=jnp.float32)
            total = term if total is None else total + term
        total = (total * jnp.where(c == 0, QUERY_SCALE, 1.0)).astype(jnp.bfloat16)
        own_ref[c] = total[:, :HEAD_DIM]
        away_ref[c] = total[:, HEAD_DIM:]
        return carry

    lax.fori_loop(0, w_ref.shape[0], step, 0)


def project(parts, tokens, w_qkv, w_parts):
    rows = sum(t.shape[0] for t in tokens)
    depth = w_qkv.shape[1]
    vmem = pl.BlockSpec(memory_space=pltpu.VMEM)
    out = jax.ShapeDtypeStruct((3, rows, HEAD_DIM), jnp.bfloat16)
    return pl.pallas_call(
        functools.partial(project_kernel, len(tokens)),
        in_specs=[pl.BlockSpec(memory_space=pltpu.SMEM)] + [vmem] * (len(tokens) + 5),
        out_specs=[vmem, vmem],
        out_shape=(out, out),
        compiler_params=pltpu.CompilerParams(vmem_limit_bytes=VMEM_BYTES),
        cost_estimate=TINY,
    )(parts, *tokens, w_qkv, *w_parts)


def attend(q, blocks, state, chunk=256):
    ones = jnp.ones((chunk, HEAD_DIM), jnp.bfloat16)
    for block in blocks:
        for at in range(0, block.shape[1], chunk):
            keys = block[1, at : at + chunk, :]
            vals = jnp.concatenate([block[2, at : at + chunk, :], ones], axis=1)
            scores = lax.dot_general(q, keys, NT, preferred_element_type=jnp.float32)
            high = jnp.max(scores, axis=1, keepdims=True)
            if state is not None:
                high = jnp.maximum(state[0], high)
            probs = jnp.exp2(scores - high).astype(jnp.bfloat16)
            term = jnp.dot(probs, vals, preferred_element_type=jnp.float32)
            if state is not None:
                term = state[1] * jnp.exp2(state[0] - high) + term
            state = (high, term)
    return state


def finished(state):
    total = state[1]
    return (total[:, :HEAD_DIM] / total[:, HEAD_DIM:]).astype(jnp.bfloat16)


def phase_kernel(n_old, n_new, last, place_ref, *refs):
    old = refs[:n_old]
    new = refs[n_old : n_old + n_new]
    refs = refs[n_old + n_new :]
    q_all = refs[-1]
    rows = new[0].shape[1]
    for i, block in enumerate(old + new):
        q_all[i * rows : (i + 1) * rows, :] = block[0]
    owned = rows // 2
    run = owned // 2
    if n_old:
        top_ref, total_ref = refs[:2]
        refs = refs[2:]

    def put(at, state):
        size = state[1].shape[0]
        if last:
            outputs = finished(state)
            for i in range(size // run):
                piece = at // run + i
                to = place_ref[piece // 2] * owned + piece % 2 * run
                here = pl.ds(pl.multiple_of(to, run), run)
                refs[0][here, :] = outputs[i * run : (i + 1) * run]
        else:
            refs[0][pl.ds(at, size), :] = jnp.broadcast_to(state[0], (size, HEAD_DIM))
            refs[1][pl.ds(at, size), :] = state[1]

    def sweep(first, count, blocks, resumed):
        tiles = next(t for t in (1, 2, 4, 8) if count * rows // t <= 1280)
        size = count * rows // tiles

        def step(t, carry):
            at = pl.multiple_of(first * rows + t * size, run)
            here = pl.ds(at, size)
            state = None
            if resumed:
                state = (jnp.max(top_ref[here, :], axis=1, keepdims=True), total_ref[here, :])
            put(at, attend(q_all[here, :], blocks, state))
            return carry

        lax.fori_loop(0, tiles, step, 0)

    if n_old:
        sweep(0, n_old, new, True)
    sweep(n_old, n_new, old + new, False)


def phase(place, old, new, state, last):
    blocks = list(old) + list(new)
    tokens = sum(b.shape[1] for b in blocks)
    vmem = pl.BlockSpec(memory_space=pltpu.VMEM)
    if last:
        out_shape = [jax.ShapeDtypeStruct((tokens, HEAD_DIM), jnp.bfloat16)]
    else:
        out_shape = [
            jax.ShapeDtypeStruct((tokens, HEAD_DIM), jnp.float32),
            jax.ShapeDtypeStruct((tokens, 2 * HEAD_DIM), jnp.float32),
        ]
    return pl.pallas_call(
        functools.partial(phase_kernel, len(old), len(new), last),
        in_specs=[pl.BlockSpec(memory_space=pltpu.SMEM)] + [vmem] * (len(blocks) + len(state)),
        out_specs=[vmem] * len(out_shape),
        out_shape=out_shape,
        scratch_shapes=[pltpu.VMEM((tokens, HEAD_DIM), jnp.bfloat16)],
        compiler_params=pltpu.CompilerParams(vmem_limit_bytes=VMEM_BYTES),
        cost_estimate=TINY,
    )(place, *blocks, *state)


def update_kernel(att_ref, noisy_ref, w_ref, out_ref):
    heads, tokens, width = att_ref.shape
    squares = jnp.zeros((tokens, width), jnp.float32)
    for h in range(heads):
        values = att_ref[h].astype(jnp.float32)
        squares += values * values
    mean = jnp.sum(squares, axis=1, keepdims=True) / (heads * width)
    gain = lax.rsqrt(mean + 1e-06)
    predicted = jnp.zeros((w_ref.shape[0], tokens), jnp.float32)
    for h in range(heads):
        normed = (att_ref[h].astype(jnp.float32) * gain).astype(jnp.bfloat16)
        predicted += lax.dot_general(
            w_ref[:, h * width : (h + 1) * width], normed, NT, preferred_element_type=jnp.float32
        )
    half = predicted.shape[0] // 2
    both = jnp.concatenate([predicted[:half], predicted[half:]], axis=1)
    parts = []
    for _ in range(3):
        part = both.astype(jnp.bfloat16)
        both = both - part.astype(jnp.float32)
        parts.append(part)
    token = lax.broadcasted_iota(jnp.int32, (2 * tokens, 2 * tokens), 0)
    column = lax.broadcasted_iota(jnp.int32, (2 * tokens, 2 * tokens), 1)
    spread = jnp.where(token < tokens, 2 * token, 2 * token - 2 * tokens + 1) == column
    spread = jnp.where(spread, 1.0, 0.0).astype(jnp.bfloat16)
    grid = jnp.dot(jnp.concatenate(parts, axis=0), spread, preferred_element_type=jnp.float32)
    grid = grid[:half] + grid[half : 2 * half] + grid[2 * half :]
    channels = half // 2
    frames = 2 * tokens // 128
    for dy in range(2):
        for f in range(frames):
            at = (dy * frames + f) * channels
            rows = grid[dy * channels : (dy + 1) * channels, f * 128 : (f + 1) * 128]
            noisy = noisy_ref[at : at + channels, :].astype(jnp.float32)
            updated = (noisy + rows).astype(jnp.bfloat16)
            for i in range(out_ref.shape[0]):
                out_ref[i, at : at + channels, :] = updated


def update_rows(by_head, noisy, w_out, copies):
    channels, frames, rows, columns = noisy.shape
    noisy = noisy.transpose(2, 1, 0, 3).reshape(rows * frames * channels, columns)
    w_rows = w_out.T.reshape(channels, 2, 2, -1).transpose(2, 1, 0, 3).reshape(4 * channels, -1)
    return pl.pallas_call(
        update_kernel,
        in_specs=[pl.BlockSpec(memory_space=pltpu.VMEM)] * 3,
        out_specs=pl.BlockSpec(memory_space=pltpu.VMEM),
        out_shape=jax.ShapeDtypeStruct((copies,) + noisy.shape, jnp.bfloat16),
        compiler_params=pltpu.CompilerParams(vmem_limit_bytes=VMEM_BYTES),
        cost_estimate=TINY,
    )(by_head, noisy, w_rows)


def features_kernel(limit_ref, rows_ref, before_ref, after_ref, w_ref, b_ref, out_ref, taps):
    frames, channels = (4, 16)
    line = frames * channels
    four = jnp.concatenate([before_ref[...], rows_ref[...], after_ref[...]], axis=0)
    wide = four.astype(jnp.float32)
    lane = lax.broadcasted_iota(jnp.int32, wide.shape, 1)
    from_left = jnp.where(lane == 0, 0.0, pltpu.roll(wide, 1, 1)).astype(jnp.bfloat16)
    from_right = jnp.where(lane == 127, 0.0, pltpu.roll(wide, 127, 1)).astype(jnp.bfloat16)
    shifted = (from_left, four, from_right)
    for dt in range(3):
        for dh in range(3):
            for dw in range(3):
                tap = (dt * 3 + dh) * 3 + dw
                for f in range(frames):
                    for y in range(2):
                        at = (y + dh) * line + max(f + dt - 2, 0) * channels
                        block = (f * 2 + y) * 128
                        taps[tap * channels : (tap + 1) * channels, block : block + 128] = shifted[
                            dw
                        ][at : at + channels]
    features = lax.dot_general(
        w_ref[...], taps[...], (((0,), (0,)), ((), ())), preferred_element_type=jnp.float32
    )
    features = features + b_ref[...]
    frame = lax.broadcasted_iota(jnp.int32, features.shape, 1) // 256
    features = jnp.where(frame < limit_ref[0], features, 0.0)
    out_ref[...] = features.reshape(out_ref.shape).astype(jnp.bfloat16)


def causal_features(rows, before, after, limit, conv_w, conv_b):
    outputs, depth = conv_w.shape
    columns = rows.shape[1]
    vmem = pl.BlockSpec(memory_space=pltpu.VMEM)
    out = pl.pallas_call(
        features_kernel,
        in_specs=[pl.BlockSpec(memory_space=pltpu.SMEM)] + [vmem] * 5,
        out_specs=vmem,
        out_shape=jax.ShapeDtypeStruct((outputs, 8, columns), jnp.bfloat16),
        scratch_shapes=[pltpu.VMEM((depth, 8 * columns), jnp.bfloat16)],
        compiler_params=pltpu.CompilerParams(vmem_limit_bytes=VMEM_BYTES),
        cost_estimate=TINY,
    )(limit[None], rows, before, after, conv_w.T, conv_b[:, None])
    return out.reshape(outputs, 4, 2, columns)


def on_device(
    latent_tokens, modulation, w_qkv, w_out, noisy_latents, queue, frame_counts, conv_w, conv_b
):
    z_low = lax.axis_index("group")
    seat = lax.axis_index("seq")
    y = lax.axis_index("dp")
    x, z_high, core = (seat // 4, seat // 2 % 2, seat % 2)

    quarter = w_qkv.shape[1] // 4
    part_0 = moved(lax.dynamic_slice_in_dim(w_qkv, y * quarter, quarter, axis=1), mirrored_z)
    part_2 = lax.dynamic_slice_in_dim(w_qkv, (y + 2) % 4 * quarter, quarter, axis=1)
    parts = (y + jnp.arange(4, dtype=jnp.int32)) % 4

    values = latent_tokens[0].astype(jnp.float32)
    shift_scale = modulation[0]
    scaled = values * lax.rsqrt(jnp.mean(values * values, axis=-1, keepdims=True) + 1e-06)
    normed = (scaled * (1.0 + shift_scale[1]) + shift_scale[0]).astype(jnp.bfloat16)

    half = normed.shape[0] // 2
    from_left = moved(normed, right)
    from_right = moved(normed, left)
    swapped = moved(normed, other_core)
    part_0, part_2, swapped = lax.optimization_barrier((part_0, part_2, swapped))
    part_1 = moved(part_0, lambda x, y, z, core: (x, y - 1, z, core))
    part_3 = moved(part_0, lambda x, y, z, core: (x, y + 1, z, core))
    part_2 = moved(part_2, mirrored_z)
    from_left, from_right, part_1, part_2, part_3 = lax.optimization_barrier(
        (from_left, from_right, part_1, part_2, part_3)
    )
    w_parts = (part_0, part_1, part_2, part_3)

    def projected(*both):
        own, away = project(parts, both, w_qkv, w_parts)
        return own, moved(away, opposite_z)

    far_0 = moved(from_left[:half], right)
    far_1 = moved(from_right[half:], left)
    own_0, away_0 = projected(normed, swapped)
    own_1, away_1 = projected(from_left, moved(from_left, other_core))
    own_2, away_2 = projected(from_right, moved(from_right, other_core))
    far_0, far_1, away_0, own_1, own_2 = lax.optimization_barrier(
        (far_0, far_1, away_0, own_1, own_2)
    )
    both = (far_0, far_1, moved(far_0, other_core), moved(far_1, other_core))
    own_3, away_3 = project(parts, both, w_qkv, w_parts)

    places = []
    early = [own_0, own_1, own_2, own_3, away_0]
    for step, z_of in zip((0, 3, 1, 2, 0, 3, 1, 2), (z_high,) * 4 + (1 - z_high,) * 4):
        for core_of in (core, 1 - core):
            places.append((((x + step) % XS) * 2 + z_of) * 2 + core_of)
    place = jnp.stack(places).astype(jnp.int32)
    state = phase(place, [], early, [], False)
    away_3, state = lax.optimization_barrier((away_3, state))
    away_3 = moved(away_3, opposite_z)
    state = phase(place, early, [away_1, away_2], state, False)
    (head_outputs,) = phase(place, early + [away_1, away_2], [away_3], state, True)

    tokens = latent_tokens.shape[1]
    by_head = lax.all_to_all(
        head_outputs.reshape(-1, tokens, HEAD_DIM), "seq", split_axis=0, concat_axis=0, tiled=True
    )
    attended = by_head.transpose(1, 0, 2).reshape(1, tokens, -1)
    new_rows = update_rows(by_head, noisy_latents[0], w_out, 2 * YS)

    slot_index = z_low * YS + y
    source = lax.dynamic_index_in_dim(queue, slot_index, 0, keepdims=False)
    limit = lax.dynamic_index_in_dim(frame_counts, source, 0, keepdims=False)
    everyone = lax.all_to_all(
        new_rows, ("group", "dp"), split_axis=0, concat_axis=0, tiled=True
    )
    chosen = lax.dynamic_index_in_dim(everyone, source, 0, keepdims=False)
    line = chosen.shape[0] // 2
    seats = lax.axis_size("seq")
    up = [(i, i + 1) for i in range(seats - 1)]
    before = lax.ppermute(chosen[line:], "seq", up)
    after = lax.ppermute(chosen[:line], "seq", [(j, i) for i, j in up])
    decoded = causal_features(chosen, before, after, limit, conv_w, conv_b)
    return (attended, decoded[None])


def solution(mesh):
    return jax.shard_map(
        on_device,
        mesh=mesh,
        in_specs=(
            P(("group", "dp"), "seq", None),
            P(("group", "dp"), None, None),
            P(None, None, "seq"),
            P(),
            P(("group", "dp"), None, None, "seq", None),
            P(),
            P(),
            P(),
            P(),
        ),
        out_specs=(P(("group", "dp"), "seq", None), P(("group", "dp"), None, None, "seq", None)),
        check_vma=False,
    )
```

profile of v0, /device:TPU:1, one launch (start us, length us, event | category | flops | bytes accessed | tf_op | source)
XLA Modules:
  0.0 161.0 jit_solution(925120580340694281)
XLA Ops:
  1.6 1.9 %fusion = f32[256]{0:T(256)S(1)} fusion(bf16[1,256,3072]{2,1,0:T(8,128)(2,1)} %param.9), kind=kLoop, calls=%fused_computation.2 | loop fusion | flops 2359040 | bytes 1573888 | tf_op jit(solution)/shard_map/reduce_sum | solution.py:299
  9.4 3.9 %collective-permute-start = (bf16[3,768,128]{2,1,0:T(8,128)(2,1)S(1)}, bf16[3,768,128]{2,1,0:T(8,128)(2,1)S(1)}, u32[]{:S(2)}, u32[]{:S(2)}) collective-permute-start(bf16[3,768,128]{2,1,0:T(8,128)(2,1)S(1)} %get-tuple-element.61), channel_id=1, source_target_pairs={{0,72},{4,76},{64,8},{68,12},{8,64},{12,68},{72,0},{76,4},{1,73},{... | collective-permute-start | bytes 1769480 | tf_op jit(solution)/shard_map/ppermute | solution.py:33
  13.4 13.3 %collective-permute-done.refs_3_.refs_5_ = bf16[3,768,128]{2,1,0:T(8,128)(2,1)S(1)} collective-permute-done((bf16[3,768,128]{2,1,0:T(8,128)(2,1)S(1)}, bf16[3,768,128]{2,1,0:T(8,128)(2,1)S(1)}, u32[]{:S(2)}, u32[]{:S(2)}) %collective-permute-start) | collective-permute-done | bytes 589856 | tf_op jit(solution)/shard_map/ppermute | solution.py:33
  26.6 2.7 %collective-permute-start.4 = (bf16[3,768,128]{2,1,0:T(8,128)(2,1)S(1)}, bf16[3,768,128]{2,1,0:T(8,128)(2,1)S(1)}, u32[]{:S(2)}, u32[]{:S(2)}) collective-permute-start(bf16[3,768,128]{2,1,0:T(8,128)(2,1)S(1)} %collective-permute-done.refs_3_.refs_5_), channel_id=1, source_target_pairs={{0,3},{4,7},{64,67},{68,71},{8,11},{12,15},{72,75},{76,79},{1,0},{... | collective-permute-start | bytes 1769480 | tf_op jit(solution)/shard_map/ppermute | solution.py:33
  29.4 2.4 %collective-permute-start.5 = (bf16[3,768,128]{2,1,0:T(8,128)(2,1)S(1)}, bf16[3,768,128]{2,1,0:T(8,128)(2,1)S(1)}, u32[]{:S(2)}, u32[]{:S(2)}) collective-permute-start(bf16[3,768,128]{2,1,0:T(8,128)(2,1)S(1)} %get-tuple-element.32), channel_id=1, source_target_pairs={{0,72},{4,76},{64,8},{68,12},{8,64},{12,68},{72,0},{76,4},{1,73},{... | collective-permute-start | bytes 1769480 | tf_op jit(solution)/shard_map/ppermute | solution.py:33
  31.7 12.5 %collective-permute-done.2.refs_0_ = bf16[256,3072]{1,0:T(8,128)(2,1)} collective-permute-done((bf16[256,3072]{1,0:T(8,128)(2,1)}, bf16[256,3072]{1,0:T(8,128)(2,1)}, u32[]{:S(2)}, u32[]{:S(2)}) %collective-permute-start.2) | collective-permute-done | bytes 1572896 | tf_op jit(solution)/shard_map/ppermute | solution.py:33
  45.9 2.8 %collective-permute-start.10 = (bf16[256,3072]{1,0:T(8,128)(2,1)}, bf16[256,3072]{1,0:T(8,128)(2,1)S(1)}, u32[]{:S(2)}, u32[]{:S(2)}) collective-permute-start(bf16[256,3072]{1,0:T(8,128)(2,1)} %collective-permute-done.2.refs_0_), channel_id=1, source_target_pairs={{0,4},{4,0},{64,68},{68,64},{8,12},{12,8},{72,76},{76,72},{1,5},{5... | collective-permute-start | bytes 4718600 | tf_op jit(solution)/shard_map/ppermute | solution.py:33
  51.2 2.7 %collective-permute-start.8 = (bf16[128,3072]{1,0:T(8,128)(2,1)S(1)}, bf16[128,3072]{1,0:T(8,128)(2,1)}, u32[]{:S(2)}, u32[]{:S(2)}) collective-permute-start(bf16[128,3072]{1,0:T(8,128)(2,1)S(1)} %slice.29), channel_id=1, source_target_pairs={{0,48},{4,52},{64,112},{68,116},{8,56},{12,60},{72,120},{76,124},{... | collective-permute-start | bytes 2359304 | tf_op jit(solution)/shard_map/ppermute | solution.py:33
  53.8 4.9 %shard_map.104 = (bf16[3,512,128]{2,1,0:T(8,128)(2,1)S(1)}, bf16[3,512,128]{2,1,0:T(8,128)(2,1)S(1)}) custom-call(s32[4]{0:T(128)S(1)} %and_select_fusion.part_ref, bf16[256,3072]{1,0:T(8,128)(2,1)} %fusion.3.refs_0_, bf16[256,3072]{1,0:T(8,128)(2,1)} %collective-permute-done.1.refs_1_, bf16[3,3072,128]{2,1,0:T(8,128)(2,1)S(1)} %copy-done, ...), custom_call_target="tpu_custom_call" | custom-call | flops 1 | bytes 1 | tf_op jit(solution)/shard_map/pallas_call | solution.py:84
  59.1 4.4 %shard_map.105 = (bf16[3,512,128]{2,1,0:T(8,128)(2,1)S(1)}, bf16[3,512,128]{2,1,0:T(8,128)(2,1)S(1)}) custom-call(s32[4]{0:T(128)S(1)} %and_select_fusion.part_ref, bf16[256,3072]{1,0:T(8,128)(2,1)} %collective-permute-done.2.refs_0_, bf16[256,3072]{1,0:T(8,128)(2,1)S(1)} %collective-permute-done.10.refs_1_, bf16[3,3072,128]{2,1,0:T(8,128)(2,1)S(1)} %copy-done, ...), custom_call_target="tpu_custom_call" | custom-call | flops 1 | bytes 1 | tf_op jit(solution)/shard_map/pallas_call | solution.py:84
  64.3 4.6 %shard_map.106 = (bf16[3,512,128]{2,1,0:T(8,128)(2,1)S(1)}, bf16[3,512,128]{2,1,0:T(8,128)(2,1)S(1)}) custom-call(s32[4]{0:T(128)S(1)} %and_select_fusion.part_ref, bf16[256,3072]{1,0:T(8,128)(2,1)} %collective-permute-done.3.refs_0_, bf16[256,3072]{1,0:T(8,128)(2,1)S(1)} %collective-permute-done.11.refs_1_, bf16[3,3072,128]{2,1,0:T(8,128)(2,1)S(1)} %copy-done, ...), custom_call_target="tpu_custom_call" | custom-call | flops 1 | bytes 1 | tf_op jit(solution)/shard_map/pallas_call | solution.py:84
  72.8 2.7 %collective-permute-start.14 = (bf16[3,512,128]{2,1,0:T(8,128)(2,1)}, bf16[3,512,128]{2,1,0:T(8,128)(2,1)S(1)}, u32[]{:S(2)}, u32[]{:S(2)}) collective-permute-start(bf16[3,512,128]{2,1,0:T(8,128)(2,1)} %copy-done.14), channel_id=1, source_target_pairs={{0,8},{4,12},{64,72},{68,76},{8,0},{12,4},{72,64},{76,68},{1,9},{5... | collective-permute-start | bytes 1179656 | tf_op jit(solution)/shard_map/ppermute | solution.py:33
  78.1 5.0 %shard_map.107 = (bf16[3,512,128]{2,1,0:T(8,128)(2,1)S(1)}, bf16[3,512,128]{2,1,0:T(8,128)(2,1)S(1)}) custom-call(s32[4]{0:T(128)S(1)} %and_select_fusion.part_ref, bf16[128,3072]{1,0:T(8,128)(2,1)} %collective-permute-done.7.refs_0_, bf16[128,3072]{1,0:T(8,128)(2,1)} %collective-permute-done.8.refs_1_, bf16[128,3072]{1,0:T(8,128)(2,1)} %collective-permute-done.12.refs_2_, ...), custom_call_target="tpu_custom_call" | custom-call | flops 1 | bytes 1 | tf_op jit(solution)/shard_map/pallas_call | solution.py:84
  83.2 8.4 %shard_map.108 = (f32[2560,128]{1,0:T(8,128)S(1)}, f32[2560,256]{1,0:T(8,128)S(1)}) custom-call(s32[16]{0:T(128)S(1)} %stack.67.place_ref, bf16[3,512,128]{2,1,0:T(8,128)(2,1)S(1)} %copy-done.6, bf16[3,512,128]{2,1,0:T(8,128)(2,1)S(1)} %copy-done.10, bf16[3,512,128]{2,1,0:T(8,128)(2,1)S(1)} %copy-done.12, ...), custom_call_target="tpu_custom_call" | custom-call | flops 1 | bytes 1 | tf_op jit(solution)/shard_map/pallas_call | solution.py:175
  91.5 2.7 %collective-permute-start.16 = (bf16[3,512,128]{2,1,0:T(8,128)(2,1)S(1)}, bf16[3,512,128]{2,1,0:T(8,128)(2,1)S(1)}, u32[]{:S(2)}, u32[]{:S(2)}) collective-permute-start(bf16[3,512,128]{2,1,0:T(8,128)(2,1)S(1)} %get-tuple-element.53), channel_id=1, source_target_pairs={{0,8},{4,12},{64,72},{68,76},{8,0},{12,4},{72,64},{76,68},{1,9},{5... | collective-permute-start | bytes 1179656 | tf_op jit(solution)/shard_map/ppermute | solution.py:33
  94.2 8.5 %shard_map.109 = (f32[3584,128]{1,0:T(8,128)S(1)}, f32[3584,256]{1,0:T(8,128)S(1)}) custom-call(s32[16]{0:T(128)S(1)} %stack.67.place_ref, bf16[3,512,128]{2,1,0:T(8,128)(2,1)S(1)} %copy-done.6, bf16[3,512,128]{2,1,0:T(8,128)(2,1)S(1)} %copy-done.10, bf16[3,512,128]{2,1,0:T(8,128)(2,1)S(1)} %copy-done.12, ...), custom_call_target="tpu_custom_call" | custom-call | flops 1 | bytes 1 | tf_op jit(solution)/shard_map/pallas_call | solution.py:175
  102.9 7.8 %shard_map.110 = bf16[4096,128]{1,0:T(8,128)(2,1)} custom-call(s32[16]{0:T(128)S(1)} %stack.67.place_ref, bf16[3,512,128]{2,1,0:T(8,128)(2,1)S(1)} %copy-done.6, bf16[3,512,128]{2,1,0:T(8,128)(2,1)S(1)} %copy-done.10, bf16[3,512,128]{2,1,0:T(8,128)(2,1)S(1)} %copy-done.12, bf16[3,512,128]{2,1,0:T(8,128)(2,1)S(1)} %get-tuple-element.46.refs_3_, ...), custom_call_target="tpu_custom_call" | custom-call | flops 1 | bytes 1 | tf_op jit(solution)/shard_map/pallas_call | solution.py:175
  110.7 6.0 %all-to-all-start = ((bf16[16,256,128]{2,1,0:T(8,128)(2,1)}), bf16[16,256,128]{2,1,0:T(8,128)(2,1)S(1)}, u32[]{:S(2)}, u32[]{:S(2)}) async-start(bf16[16,256,128]{2,1,0:T(8,128)(2,1)} %bitcast.20), calls=%async_computation | async-start | bytes 2097152 | tf_op jit(solution)/shard_map/all_to_all | solution.py:343
  117.1 16.8 %all-to-all-done.att_ref = bf16[16,256,128]{2,1,0:T(8,128)(2,1)S(1)} async-done(((bf16[16,256,128]{2,1,0:T(8,128)(2,1)}), bf16[16,256,128]{2,1,0:T(8,128)(2,1)S(1)}, u32[]{:S(2)}, u32[]{:S(2)}) %all-to-all-start) | async-done | bytes 1048608 | tf_op jit(solution)/shard_map/all_to_all | solution.py:343
  135.7 4.6 %all-to-all-start.1 = ((bf16[8,128,128]{2,1,0:T(8,128)(2,1)}), bf16[8,128,128]{2,1,0:T(8,128)(2,1)S(1)}, u32[]{:S(2)}, u32[]{:S(2)}) async-start(bf16[8,128,128]{2,1,0:T(8,128)(2,1)} %shard_map.111), calls=%async_computation.1 | async-start | bytes 524288 | tf_op jit(solution)/shard_map/all_to_all | solution.py:352
  146.7 4.9 %collective-permute-start.17 = (bf16[64,128]{1,0:T(8,128)(2,1)S(1)}, bf16[64,128]{1,0:T(8,128)(2,1)S(1)}, u32[]{:S(2)}, u32[]{:S(2)}) collective-permute-start(bf16[64,128]{1,0:T(8,128)(2,1)S(1)} %get-tuple-element.63), channel_id=1, source_target_pairs={{0,4},{4,8},{8,12},{12,16},{16,20},{20,24},{24,28},{28,32},{32,36}... | collective-permute-start | bytes 49160 | tf_op jit(solution)/shard_map/ppermute | solution.py:359
  151.7 1.9 %collective-permute-start.18 = (bf16[64,128]{1,0:T(8,128)(2,1)S(1)}, bf16[64,128]{1,0:T(8,128)(2,1)S(1)}, u32[]{:S(2)}, u32[]{:S(2)}) collective-permute-start(bf16[64,128]{1,0:T(8,128)(2,1)S(1)} %get-tuple-element.62), channel_id=1, source_target_pairs={{4,0},{8,4},{12,8},{16,12},{20,16},{24,20},{28,24},{32,28},{36,32}... | collective-permute-start | bytes 49160 | tf_op jit(solution)/shard_map/ppermute | solution.py:360
  153.6 4.6 %collective-permute-done.18.after_ref = bf16[64,128]{1,0:T(8,128)(2,1)S(1)} collective-permute-done((bf16[64,128]{1,0:T(8,128)(2,1)S(1)}, bf16[64,128]{1,0:T(8,128)(2,1)S(1)}, u32[]{:S(2)}, u32[]{:S(2)}) %collective-permute-start.18) | collective-permute-done | bytes 16416 | tf_op jit(solution)/shard_map/ppermute | solution.py:360
  158.2 2.7 %shard_map.112 = bf16[512,8,128]{2,1,0:T(8,128)(2,1)} custom-call(s32[1]{0:T(128)} %dynamic_slice.20.limit_ref, bf16[128,128]{1,0:T(8,128)(2,1)S(1)} %dynamic-slice_bitcast_fusion.rows_ref, bf16[64,128]{1,0:T(8,128)(2,1)S(1)} %collective-permute-done.17.before_ref, bf16[64,128]{1,0:T(8,128)(2,1)S(1)} %collective-permute-done.18.after_ref, ...), custom_call_target="tpu_custom_call" | custom-call | flops 1 | bytes 1 | tf_op jit(solution)/shard_map/pallas_call | solution.py:272
  (90 shorter events, 25.4 us)
Async XLA Ops:
  5.3 21.4 %collective-permute-start.1 = (bf16[256,3072]{1,0:T(8,128)(2,1)}, bf16[256,3072]{1,0:T(8,128)(2,1)}, u32[]{:S(2)}, u32[]{:S(2)}) collective-permute-start(bf16[256,3072]{1,0:T(8,128)(2,1)} %fusion.3.refs_0_), channel_id=1, source_target_pairs={{0,4},{4,0},{64,68},{68,64},{8,12},{12,8},{72,76},{76,72},{1,5},{5... | collective-permute-start | bytes 4718600 | tf_op jit(solution)/shard_map/ppermute | solution.py:33
  6.7 37.6 %collective-permute-start.2 = (bf16[256,3072]{1,0:T(8,128)(2,1)}, bf16[256,3072]{1,0:T(8,128)(2,1)}, u32[]{:S(2)}, u32[]{:S(2)}) collective-permute-start(bf16[256,3072]{1,0:T(8,128)(2,1)} %fusion.3.refs_0_), channel_id=1, source_target_pairs={{0,16},{4,20},{64,80},{68,84},{8,24},{12,28},{72,88},{76,92},{1,17... | collective-permute-start | bytes 4718600 | tf_op jit(solution)/shard_map/ppermute | solution.py:33
  8.0 36.3 %collective-permute-start.3 = (bf16[256,3072]{1,0:T(8,128)(2,1)}, bf16[256,3072]{1,0:T(8,128)(2,1)}, u32[]{:S(2)}, u32[]{:S(2)}) collective-permute-start(bf16[256,3072]{1,0:T(8,128)(2,1)} %fusion.3.refs_0_), channel_id=1, source_target_pairs={{0,48},{4,52},{64,112},{68,116},{8,56},{12,60},{72,120},{76,124},{... | collective-permute-start | bytes 4718600 | tf_op jit(solution)/shard_map/ppermute | solution.py:33
  9.4 17.2 %collective-permute-start = (bf16[3,768,128]{2,1,0:T(8,128)(2,1)S(1)}, bf16[3,768,128]{2,1,0:T(8,128)(2,1)S(1)}, u32[]{:S(2)}, u32[]{:S(2)}) collective-permute-start(bf16[3,768,128]{2,1,0:T(8,128)(2,1)S(1)} %get-tuple-element.61), channel_id=1, source_target_pairs={{0,72},{4,76},{64,8},{68,12},{8,64},{12,68},{72,0},{76,4},{1,73},{... | collective-permute-start | bytes 1769480 | tf_op jit(solution)/shard_map/ppermute | solution.py:33
  26.6 17.6 %collective-permute-start.4 = (bf16[3,768,128]{2,1,0:T(8,128)(2,1)S(1)}, bf16[3,768,128]{2,1,0:T(8,128)(2,1)S(1)}, u32[]{:S(2)}, u32[]{:S(2)}) collective-permute-start(bf16[3,768,128]{2,1,0:T(8,128)(2,1)S(1)} %collective-permute-done.refs_3_.refs_5_), channel_id=1, source_target_pairs={{0,3},{4,7},{64,67},{68,71},{8,11},{12,15},{72,75},{76,79},{1,0},{... | collective-permute-start | bytes 1769480 | tf_op jit(solution)/shard_map/ppermute | solution.py:33
  29.4 14.9 %collective-permute-start.5 = (bf16[3,768,128]{2,1,0:T(8,128)(2,1)S(1)}, bf16[3,768,128]{2,1,0:T(8,128)(2,1)S(1)}, u32[]{:S(2)}, u32[]{:S(2)}) collective-permute-start(bf16[3,768,128]{2,1,0:T(8,128)(2,1)S(1)} %get-tuple-element.32), channel_id=1, source_target_pairs={{0,72},{4,76},{64,8},{68,12},{8,64},{12,68},{72,0},{76,4},{1,73},{... | collective-permute-start | bytes 1769480 | tf_op jit(solution)/shard_map/ppermute | solution.py:33
  31.7 14.2 %collective-permute-start.6 = (bf16[3,768,128]{2,1,0:T(8,128)(2,1)S(1)}, bf16[3,768,128]{2,1,0:T(8,128)(2,1)S(1)}, u32[]{:S(2)}, u32[]{:S(2)}) collective-permute-start(bf16[3,768,128]{2,1,0:T(8,128)(2,1)S(1)} %collective-permute-done.refs_3_.refs_5_), channel_id=1, source_target_pairs={{0,1},{4,5},{64,65},{68,69},{8,9},{12,13},{72,73},{76,77},{1,2},{5... | collective-permute-start | bytes 1769480 | tf_op jit(solution)/shard_map/ppermute | solution.py:33
  45.9 13.2 %collective-permute-start.10 = (bf16[256,3072]{1,0:T(8,128)(2,1)}, bf16[256,3072]{1,0:T(8,128)(2,1)S(1)}, u32[]{:S(2)}, u32[]{:S(2)}) collective-permute-start(bf16[256,3072]{1,0:T(8,128)(2,1)} %collective-permute-done.2.refs_0_), channel_id=1, source_target_pairs={{0,4},{4,0},{64,68},{68,64},{8,12},{12,8},{72,76},{76,72},{1,5},{5... | collective-permute-start | bytes 4718600 | tf_op jit(solution)/shard_map/ppermute | solution.py:33
  48.7 15.6 %collective-permute-start.11 = (bf16[256,3072]{1,0:T(8,128)(2,1)}, bf16[256,3072]{1,0:T(8,128)(2,1)S(1)}, u32[]{:S(2)}, u32[]{:S(2)}) collective-permute-start(bf16[256,3072]{1,0:T(8,128)(2,1)} %collective-permute-done.3.refs_0_), channel_id=1, source_target_pairs={{0,4},{4,0},{64,68},{68,64},{8,12},{12,8},{72,76},{76,72},{1,5},{5... | collective-permute-start | bytes 4718600 | tf_op jit(solution)/shard_map/ppermute | solution.py:33
  51.1 20.1 %collective-permute-start.7 = (bf16[128,3072]{1,0:T(8,128)(2,1)S(1)}, bf16[128,3072]{1,0:T(8,128)(2,1)}, u32[]{:S(2)}, u32[]{:S(2)}) collective-permute-start(bf16[128,3072]{1,0:T(8,128)(2,1)S(1)} %slice.28), channel_id=1, source_target_pairs={{0,16},{4,20},{64,80},{68,84},{8,24},{12,28},{72,88},{76,92},{1,17... | collective-permute-start | bytes 2359304 | tf_op jit(solution)/shard_map/ppermute | solution.py:33
  51.2 20.0 %collective-permute-start.8 = (bf16[128,3072]{1,0:T(8,128)(2,1)S(1)}, bf16[128,3072]{1,0:T(8,128)(2,1)}, u32[]{:S(2)}, u32[]{:S(2)}) collective-permute-start(bf16[128,3072]{1,0:T(8,128)(2,1)S(1)} %slice.29), channel_id=1, source_target_pairs={{0,48},{4,52},{64,112},{68,116},{8,56},{12,60},{72,120},{76,124},{... | collective-permute-start | bytes 2359304 | tf_op jit(solution)/shard_map/ppermute | solution.py:33
  58.7 11.7 %collective-permute-start.9 = (bf16[3,512,128]{2,1,0:T(8,128)(2,1)S(1)}, bf16[3,512,128]{2,1,0:T(8,128)(2,1)S(1)}, u32[]{:S(2)}, u32[]{:S(2)}) collective-permute-start(bf16[3,512,128]{2,1,0:T(8,128)(2,1)S(1)} %get-tuple-element.39), channel_id=1, source_target_pairs={{0,8},{4,12},{64,72},{68,76},{8,0},{12,4},{72,64},{76,68},{1,9},{5... | collective-permute-start | bytes 1179656 | tf_op jit(solution)/shard_map/ppermute | solution.py:33
  71.2 4.7 %collective-permute-start.12 = (bf16[128,3072]{1,0:T(8,128)(2,1)}, bf16[128,3072]{1,0:T(8,128)(2,1)}, u32[]{:S(2)}, u32[]{:S(2)}) collective-permute-start(bf16[128,3072]{1,0:T(8,128)(2,1)} %collective-permute-done.7.refs_0_), channel_id=1, source_target_pairs={{0,4},{4,0},{64,68},{68,64},{8,12},{12,8},{72,76},{76,72},{1,5},{5... | collective-permute-start | bytes 2359304 | tf_op jit(solution)/shard_map/ppermute | solution.py:33
  72.6 3.4 %collective-permute-start.13 = (bf16[128,3072]{1,0:T(8,128)(2,1)}, bf16[128,3072]{1,0:T(8,128)(2,1)}, u32[]{:S(2)}, u32[]{:S(2)}) collective-permute-start(bf16[128,3072]{1,0:T(8,128)(2,1)} %collective-permute-done.8.refs_1_), channel_id=1, source_target_pairs={{0,4},{4,0},{64,68},{68,64},{8,12},{12,8},{72,76},{76,72},{1,5},{5... | collective-permute-start | bytes 2359304 | tf_op jit(solution)/shard_map/ppermute | solution.py:33
  72.8 21.4 %collective-permute-start.14 = (bf16[3,512,128]{2,1,0:T(8,128)(2,1)}, bf16[3,512,128]{2,1,0:T(8,128)(2,1)S(1)}, u32[]{:S(2)}, u32[]{:S(2)}) collective-permute-start(bf16[3,512,128]{2,1,0:T(8,128)(2,1)} %copy-done.14), channel_id=1, source_target_pairs={{0,8},{4,12},{64,72},{68,76},{8,0},{12,4},{72,64},{76,68},{1,9},{5... | collective-permute-start | bytes 1179656 | tf_op jit(solution)/shard_map/ppermute | solution.py:33
  75.5 18.7 %collective-permute-start.15 = (bf16[3,512,128]{2,1,0:T(8,128)(2,1)}, bf16[3,512,128]{2,1,0:T(8,128)(2,1)S(1)}, u32[]{:S(2)}, u32[]{:S(2)}) collective-permute-start(bf16[3,512,128]{2,1,0:T(8,128)(2,1)} %copy-done.15), channel_id=1, source_target_pairs={{0,8},{4,12},{64,72},{68,76},{8,0},{12,4},{72,64},{76,68},{1,9},{5... | collective-permute-start | bytes 1179656 | tf_op jit(solution)/shard_map/ppermute | solution.py:33
  91.5 11.4 %collective-permute-start.16 = (bf16[3,512,128]{2,1,0:T(8,128)(2,1)S(1)}, bf16[3,512,128]{2,1,0:T(8,128)(2,1)S(1)}, u32[]{:S(2)}, u32[]{:S(2)}) collective-permute-start(bf16[3,512,128]{2,1,0:T(8,128)(2,1)S(1)} %get-tuple-element.53), channel_id=1, source_target_pairs={{0,8},{4,12},{64,72},{68,76},{8,0},{12,4},{72,64},{76,68},{1,9},{5... | collective-permute-start | bytes 1179656 | tf_op jit(solution)/shard_map/ppermute | solution.py:33
  110.7 29.5 %copy-start.20 = (s32[8]{0:T(128)S(1)}, s32[8]{0:T(128)}, u32[]{:S(2)}) copy-start(s32[8]{0:T(128)} %param.14) | copy-start | bytes 100
  110.7 31.4 %copy-start.19 = (f32[512]{0:T(512)S(1)}, f32[512]{0:T(512)}, u32[]{:S(2)}) copy-start(f32[512]{0:T(512)} %param.17) | copy-start | bytes 6148
  110.7 32.3 %copy-start.21 = (s32[8]{0:T(128)S(1)}, s32[8]{0:T(128)}, u32[]{:S(2)}) copy-start(s32[8]{0:T(128)} %param.15) | copy-start | bytes 100
  110.7 23.2 %all-to-all-start = ((bf16[16,256,128]{2,1,0:T(8,128)(2,1)}), bf16[16,256,128]{2,1,0:T(8,128)(2,1)S(1)}, u32[]{:S(2)}, u32[]{:S(2)}) async-start(bf16[16,256,128]{2,1,0:T(8,128)(2,1)} %bitcast.20), calls=%async_computation | async-start | bytes 2097152 | tf_op jit(solution)/shard_map/all_to_all | solution.py:343
  135.7 11.0 %all-to-all-start.1 = ((bf16[8,128,128]{2,1,0:T(8,128)(2,1)}), bf16[8,128,128]{2,1,0:T(8,128)(2,1)S(1)}, u32[]{:S(2)}, u32[]{:S(2)}) async-start(bf16[8,128,128]{2,1,0:T(8,128)(2,1)} %shard_map.111), calls=%async_computation.1 | async-start | bytes 524288 | tf_op jit(solution)/shard_map/all_to_all | solution.py:352
  146.7 6.9 %collective-permute-start.17 = (bf16[64,128]{1,0:T(8,128)(2,1)S(1)}, bf16[64,128]{1,0:T(8,128)(2,1)S(1)}, u32[]{:S(2)}, u32[]{:S(2)}) collective-permute-start(bf16[64,128]{1,0:T(8,128)(2,1)S(1)} %get-tuple-element.63), channel_id=1, source_target_pairs={{0,4},{4,8},{8,12},{12,16},{16,20},{20,24},{24,28},{28,32},{32,36}... | collective-permute-start | bytes 49160 | tf_op jit(solution)/shard_map/ppermute | solution.py:359
  151.7 6.6 %collective-permute-start.18 = (bf16[64,128]{1,0:T(8,128)(2,1)S(1)}, bf16[64,128]{1,0:T(8,128)(2,1)S(1)}, u32[]{:S(2)}, u32[]{:S(2)}) collective-permute-start(bf16[64,128]{1,0:T(8,128)(2,1)S(1)} %get-tuple-element.62), channel_id=1, source_target_pairs={{4,0},{8,4},{12,8},{16,12},{20,16},{24,20},{28,24},{32,28},{36,32}... | collective-permute-start | bytes 49160 | tf_op jit(solution)/shard_map/ppermute | solution.py:360
  (19 other events, 129.5 us)
where the time goes:
time: 162 us; the launch traced here: 161 us
  waiting for transfers between devices  50.4 us (31%)
  Pallas kernels  48 us (30%)
  starting transfers between devices  43.7 us (27%)
  local copies, waits for them, and re-layouts  11.4 us (7%)
  other arithmetic  4.6 us (3%)
  between operations  2.92 us (2%)
    ppermute x17, waiting for transfers between devices, moved(): return lax.ppermute(array, EVERY, perm)  27.8 us
    ppermute x17, starting transfers between devices, moved(): return lax.ppermute(array, EVERY, perm)  26.3 us
    pallas_call x3, Pallas kernels, phase(): pl.pallas_call(functools.partial(phase_kernel, len(old), len(new), last),...  24.7 us
    pallas_call x4, Pallas kernels, project(): pl.pallas_call(functools.partial(project_kernel, len(tokens)), in_specs=[...  18.8 us
    all_to_all x1, waiting for transfers between devices, on_device(): lax.all_to_all(head_outputs.reshape(-1, tokens, HEAD_DIM), 'seq', split_a...  16.8 us
    unnamed x45, local copies, waits for them, and re-layouts  6.62 us
    all_to_all x1, starting transfers between devices, on_device(): lax.all_to_all(head_outputs.reshape(-1, tokens, HEAD_DIM), 'seq', split_a...  6.04 us
    ppermute x1, starting transfers between devices, on_device(): before = lax.ppermute(chosen[line:], 'seq', up)  4.93 us
  transfers between devices with their start and end apart: 21, of which 8 were waited for; matrix products, arithmetic and copies ran while one was open for 4% of the time, Pallas kernels for 22%

commit v1 on v0

--- a/solution.py
+++ b/solution.py
@@ -236,48 +236,94 @@
     )(by_head, noisy, w_rows)
 
 
-def features_kernel(limit_ref, rows_ref, before_ref, after_ref, w_ref, b_ref, out_ref, taps):
-    frames, channels = (4, 16)
-    line = frames * channels
-    four = jnp.concatenate([before_ref[...], rows_ref[...], after_ref[...]], axis=0)
-    wide = four.astype(jnp.float32)
+def shifted_rows(rows):
+    wide = rows.astype(jnp.float32)
     lane = lax.broadcasted_iota(jnp.int32, wide.shape, 1)
     from_left = jnp.where(lane == 0, 0.0, pltpu.roll(wide, 1, 1)).astype(jnp.bfloat16)
     from_right = jnp.where(lane == 127, 0.0, pltpu.roll(wide, 127, 1)).astype(jnp.bfloat16)
-    shifted = (from_left, four, from_right)
+    return (from_left, rows, from_right)
+
+
+def tap_product(w_ref, taps, lines, frames, channels):
+    weights = []
+    at = 0
     for dt in range(3):
-        for dh in range(3):
+        for dh, shifted in lines:
+            first = (dt * 9 + dh * 3) * channels
+            weights.append(w_ref[first : first + 3 * channels, :])
             for dw in range(3):
-                tap = (dt * 3 + dh) * 3 + dw
                 for f in range(frames):
-                    for y in range(2):
-                        at = (y + dh) * line + max(f + dt - 2, 0) * channels
-                        block = (f * 2 + y) * 128
-                        taps[tap * channels : (tap + 1) * channels, block : block + 128] = shifted[
-                            dw
-                        ][at : at + channels]
-    features = lax.dot_general(
-        w_ref[...], taps[...], (((0,), (0,)), ((), ())), preferred_element_type=jnp.float32
-    )
-    features = features + b_ref[...]
-    frame = lax.broadcasted_iota(jnp.int32, features.shape, 1) // 256
-    features = jnp.where(frame < limit_ref[0], features, 0.0)
-    out_ref[...] = features.reshape(out_ref.shape).astype(jnp.bfloat16)
-
-
-def causal_features(rows, before, after, limit, conv_w, conv_b):
+                    source = max(f + dt - 2, 0) * channels
+                    taps[at : at + channels, f * 128 : (f + 1) * 128] = shifted[dw][
+                        source : source + channels
+                    ]
+                at += channels
+    return lax.dot_general(
+        jnp.concatenate(weights, axis=0),
+        taps[...],
+        (((0,), (0,)), ((), ())),
+        preferred_element_type=jnp.float32,
+    )
+
+
+def inner_kernel(rows_ref, w_ref, b_ref, out_ref, taps_0, taps_1):
+    line = rows_ref.shape[0] // 2
+    frames = out_ref.shape[2] // 128
+    channels = line // frames
+    upper = shifted_rows(rows_ref[:line, :])
+    lower = shifted_rows(rows_ref[line:, :])
+    for y, taps, lines in (
+        (0, taps_0, ((1, upper), (2, lower))),
+        (1, taps_1, ((0, upper), (1, lower))),
+    ):
+        out_ref[y] = tap_product(w_ref, taps, lines, frames, channels) + b_ref[...]
+
+
+def halo_kernel(limit_ref, inner_ref, before_ref, after_ref, w_ref, out_ref, taps_0, taps_1):
+    frames = inner_ref.shape[2] // 128
+    channels = before_ref.shape[0] // frames
+    features = []
+    for y, taps, dh, ref in ((0, taps_0, 0, before_ref), (1, taps_1, 2, after_ref)):
+        lines = ((dh, shifted_rows(ref[...])),)
+        features.append(inner_ref[y] + tap_product(w_ref, taps, lines, frames, channels))
+    blocks = []
+    for f in range(frames):
+        for y in range(2):
+            block = features[y][:, f * 128 : (f + 1) * 128]
+            blocks.append(jnp.where(f < limit_ref[0], block, 0.0))
+    together = jnp.concatenate(blocks, axis=1)
+    out_ref[...] = together.reshape(out_ref.shape).astype(jnp.bfloat16)
+
+
+def inner_features(rows, conv_w, conv_b):
     outputs, depth = conv_w.shape
-    columns = rows.shape[1]
     vmem = pl.BlockSpec(memory_space=pltpu.VMEM)
+    taps = pltpu.VMEM((depth * 2 // 3, 4 * rows.shape[1]), jnp.bfloat16)
+    return pl.pallas_call(
+        inner_kernel,
+        in_specs=[vmem] * 3,
+        out_specs=vmem,
+        out_shape=jax.ShapeDtypeStruct((2, outputs, 4 * rows.shape[1]), jnp.float32),
+        scratch_shapes=[taps, taps],
+        compiler_params=pltpu.CompilerParams(vmem_limit_bytes=VMEM_BYTES),
+        cost_estimate=TINY,
+    )(rows, conv_w.T, conv_b[:, None])
+
+
+def all_features(inner, before, after, limit, conv_w):
+    outputs, depth = conv_w.shape
+    columns = before.shape[1]
+    vmem = pl.BlockSpec(memory_space=pltpu.VMEM)
+    taps = pltpu.VMEM((depth // 3, 4 * columns), jnp.bfloat16)
     out = pl.pallas_call(
-        features_kernel,
-        in_specs=[pl.BlockSpec(memory_space=pltpu.SMEM)] + [vmem] * 5,
+        halo_kernel,
+        in_specs=[pl.BlockSpec(memory_space=pltpu.SMEM)] + [vmem] * 4,
         out_specs=vmem,
         out_shape=jax.ShapeDtypeStruct((outputs, 8, columns), jnp.bfloat16),
-        scratch_shapes=[pltpu.VMEM((depth, 8 * columns), jnp.bfloat16)],
+        scratch_shapes=[taps, taps],
         compiler_params=pltpu.CompilerParams(vmem_limit_bytes=VMEM_BYTES),
         cost_estimate=TINY,
-    )(limit[None], rows, before, after, conv_w.T, conv_b[:, None])
+    )(limit[None], inner, before, after, conv_w.T)
     return out.reshape(outputs, 4, 2, columns)
 
 
@@ -304,11 +350,13 @@
     from_right = moved(normed, left)
     swapped = moved(normed, other_core)
     part_0, part_2, swapped = lax.optimization_barrier((part_0, part_2, swapped))
+    part_2 = moved(part_2, mirrored_z)
     part_1 = moved(part_0, lambda x, y, z, core: (x, y - 1, z, core))
     part_3 = moved(part_0, lambda x, y, z, core: (x, y + 1, z, core))
-    part_2 = moved(part_2, mirrored_z)
-    from_left, from_right, part_1, part_2, part_3 = lax.optimization_barrier(
-        (from_left, from_right, part_1, part_2, part_3)
+    near_0 = from_left[:half]
+    near_1 = from_right[half:]
+    near_0, near_1, from_left, from_right, part_1, part_2, part_3 = lax.optimization_barrier(
+        (near_0, near_1, from_left, from_right, part_1, part_2, part_3)
     )
     w_parts = (part_0, part_1, part_2, part_3)
 
@@ -316,8 +364,8 @@
         own, away = project(parts, both, w_qkv, w_parts)
         return own, moved(away, opposite_z)
 
-    far_0 = moved(from_left[:half], right)
-    far_1 = moved(from_right[half:], left)
+    far_0 = moved(near_0, right)
+    far_1 = moved(near_1, left)
     own_0, away_0 = projected(normed, swapped)
     own_1, away_1 = projected(from_left, moved(from_left, other_core))
     own_2, away_2 = projected(from_right, moved(from_right, other_core))
@@ -358,7 +406,8 @@
     up = [(i, i + 1) for i in range(seats - 1)]
     before = lax.ppermute(chosen[line:], "seq", up)
     after = lax.ppermute(chosen[:line], "seq", [(j, i) for i, j in up])
-    decoded = causal_features(chosen, before, after, limit, conv_w, conv_b)
+    inner = inner_features(chosen, conv_w, conv_b)
+    decoded = all_features(inner, before, after, limit, conv_w)
     return (attended, decoded[None])
 
 

time: 162 us -> 161 us (level)
  transfers between devices with their start and end apart: 21 -> 21, of which waited for: 8 -> 8; matrix products, arithmetic and copies ran while one was open for 4% -> 4% of each run, Pallas kernels for 22% -> 23%
where the time goes in v1:
time: 161 us; the launch traced here: 160 us
  waiting for transfers between devices  50.1 us (31%)
  Pallas kernels  48.5 us (30%)
  starting transfers between devices  43 us (27%)
  local copies, waits for them, and re-layouts  11.4 us (7%)
  other arithmetic  4.6 us (3%)
  between operations  2.96 us (2%)
    ppermute x17, waiting for transfers between devices, moved(): return lax.ppermute(array, EVERY, perm)  28.3 us
    ppermute x17, starting transfers between devices, moved(): return lax.ppermute(array, EVERY, perm)  25.4 us
    pallas_call x3, Pallas kernels, phase(): pl.pallas_call(functools.partial(phase_kernel, len(old), len(new), last),...  24.7 us
    pallas_call x4, Pallas kernels, project(): pl.pallas_call(functools.partial(project_kernel, len(tokens)), in_specs=[...  18.9 us
    all_to_all x1, waiting for transfers between devices, on_device(): lax.all_to_all(head_outputs.reshape(-1, tokens, HEAD_DIM), 'seq', split_a...  16.8 us
    unnamed x45, local copies, waits for them, and re-layouts  6.63 us
    all_to_all x1, starting transfers between devices, on_device(): lax.all_to_all(head_outputs.reshape(-1, tokens, HEAD_DIM), 'seq', split_a...  6.05 us
    ppermute x1, starting transfers between devices, on_device(): before = lax.ppermute(chosen[line:], 'seq', up)  4.93 us
  transfers between devices with their start and end apart: 21, of which 8 were waited for; matrix products, arithmetic and copies ran while one was open for 4% of the time, Pallas kernels for 23%

profile of v1, /device:TPU:1, one launch (start us, length us, event | category | flops | bytes accessed | tf_op | source)
XLA Modules:
  0.0 160.5 jit_solution(929768412201368226)
XLA Ops:
  1.6 1.9 %fusion = f32[256]{0:T(256)S(1)} fusion(bf16[1,256,3072]{2,1,0:T(8,128)(2,1)} %param.9), kind=kLoop, calls=%fused_computation.2 | loop fusion | flops 2359040 | bytes 1573888 | tf_op jit(solution)/shard_map/reduce_sum | solution.py:345
  9.4 3.9 %collective-permute-start = (bf16[3,768,128]{2,1,0:T(8,128)(2,1)S(1)}, bf16[3,768,128]{2,1,0:T(8,128)(2,1)S(1)}, u32[]{:S(2)}, u32[]{:S(2)}) collective-permute-start(bf16[3,768,128]{2,1,0:T(8,128)(2,1)S(1)} %get-tuple-element.65), channel_id=1, source_target_pairs={{0,72},{4,76},{64,8},{68,12},{8,64},{12,68},{72,0},{76,4},{1,73},{... | collective-permute-start | bytes 1769480 | tf_op jit(solution)/shard_map/ppermute | solution.py:33
  13.4 13.3 %collective-permute-done.refs_3_.refs_5_ = bf16[3,768,128]{2,1,0:T(8,128)(2,1)S(1)} collective-permute-done((bf16[3,768,128]{2,1,0:T(8,128)(2,1)S(1)}, bf16[3,768,128]{2,1,0:T(8,128)(2,1)S(1)}, u32[]{:S(2)}, u32[]{:S(2)}) %collective-permute-start) | collective-permute-done | bytes 589856 | tf_op jit(solution)/shard_map/ppermute | solution.py:33
  26.6 2.7 %collective-permute-start.4 = (bf16[3,768,128]{2,1,0:T(8,128)(2,1)S(1)}, bf16[3,768,128]{2,1,0:T(8,128)(2,1)S(1)}, u32[]{:S(2)}, u32[]{:S(2)}) collective-permute-start(bf16[3,768,128]{2,1,0:T(8,128)(2,1)S(1)} %collective-permute-done.refs_3_.refs_5_), channel_id=1, source_target_pairs={{0,3},{4,7},{64,67},{68,71},{8,11},{12,15},{72,75},{76,79},{1,0},{... | collective-permute-start | bytes 1769480 | tf_op jit(solution)/shard_map/ppermute | solution.py:33
  29.4 2.4 %collective-permute-start.5 = (bf16[3,768,128]{2,1,0:T(8,128)(2,1)S(1)}, bf16[3,768,128]{2,1,0:T(8,128)(2,1)S(1)}, u32[]{:S(2)}, u32[]{:S(2)}) collective-permute-start(bf16[3,768,128]{2,1,0:T(8,128)(2,1)S(1)} %get-tuple-element.34), channel_id=1, source_target_pairs={{0,72},{4,76},{64,8},{68,12},{8,64},{12,68},{72,0},{76,4},{1,73},{... | collective-permute-start | bytes 1769480 | tf_op jit(solution)/shard_map/ppermute | solution.py:33
  31.7 12.5 %collective-permute-done.2.refs_0_ = bf16[256,3072]{1,0:T(8,128)(2,1)} collective-permute-done((bf16[256,3072]{1,0:T(8,128)(2,1)}, bf16[256,3072]{1,0:T(8,128)(2,1)}, u32[]{:S(2)}, u32[]{:S(2)}) %collective-permute-start.2) | collective-permute-done | bytes 1572896 | tf_op jit(solution)/shard_map/ppermute | solution.py:33
  46.7 2.0 %collective-permute-start.10 = (bf16[256,3072]{1,0:T(8,128)(2,1)}, bf16[256,3072]{1,0:T(8,128)(2,1)S(1)}, u32[]{:S(2)}, u32[]{:S(2)}) collective-permute-start(bf16[256,3072]{1,0:T(8,128)(2,1)} %collective-permute-done.2.refs_0_), channel_id=1, source_target_pairs={{0,4},{4,0},{64,68},{68,64},{8,12},{12,8},{72,76},{76,72},{1,5},{5... | collective-permute-start | bytes 4718600 | tf_op jit(solution)/shard_map/ppermute | solution.py:33
  48.7 2.7 %collective-permute-start.8 = (bf16[128,3072]{1,0:T(8,128)(2,1)S(1)}, bf16[128,3072]{1,0:T(8,128)(2,1)}, u32[]{:S(2)}, u32[]{:S(2)}) collective-permute-start(bf16[128,3072]{1,0:T(8,128)(2,1)S(1)} %slice.35), channel_id=1, source_target_pairs={{0,48},{4,52},{64,112},{68,116},{8,56},{12,60},{72,120},{76,124},{... | collective-permute-start | bytes 2359304 | tf_op jit(solution)/shard_map/ppermute | solution.py:33
  51.4 4.9 %shard_map.104 = (bf16[3,512,128]{2,1,0:T(8,128)(2,1)S(1)}, bf16[3,512,128]{2,1,0:T(8,128)(2,1)S(1)}) custom-call(s32[4]{0:T(128)S(1)} %and_select_fusion.part_ref, bf16[256,3072]{1,0:T(8,128)(2,1)} %fusion.3.refs_0_, bf16[256,3072]{1,0:T(8,128)(2,1)} %collective-permute-done.1.refs_1_, bf16[3,3072,128]{2,1,0:T(8,128)(2,1)S(1)} %copy-done, ...), custom_call_target="tpu_custom_call" | custom-call | flops 1 | bytes 1 | tf_op jit(solution)/shard_map/pallas_call | solution.py:84
  56.3 2.7 %collective-permute-start.9 = (bf16[3,512,128]{2,1,0:T(8,128)(2,1)S(1)}, bf16[3,512,128]{2,1,0:T(8,128)(2,1)S(1)}, u32[]{:S(2)}, u32[]{:S(2)}) collective-permute-start(bf16[3,512,128]{2,1,0:T(8,128)(2,1)S(1)} %get-tuple-element.41), channel_id=1, source_target_pairs={{0,8},{4,12},{64,72},{68,76},{8,0},{12,4},{72,64},{76,68},{1,9},{5... | collective-permute-start | bytes 1179656 | tf_op jit(solution)/shard_map/ppermute | solution.py:33
  59.0 4.4 %shard_map.105 = (bf16[3,512,128]{2,1,0:T(8,128)(2,1)S(1)}, bf16[3,512,128]{2,1,0:T(8,128)(2,1)S(1)}) custom-call(s32[4]{0:T(128)S(1)} %and_select_fusion.part_ref, bf16[256,3072]{1,0:T(8,128)(2,1)} %collective-permute-done.2.refs_0_, bf16[256,3072]{1,0:T(8,128)(2,1)S(1)} %collective-permute-done.10.refs_1_, bf16[3,3072,128]{2,1,0:T(8,128)(2,1)S(1)} %copy-done, ...), custom_call_target="tpu_custom_call" | custom-call | flops 1 | bytes 1 | tf_op jit(solution)/shard_map/pallas_call | solution.py:84
  64.2 4.6 %shard_map.106 = (bf16[3,512,128]{2,1,0:T(8,128)(2,1)S(1)}, bf16[3,512,128]{2,1,0:T(8,128)(2,1)S(1)}) custom-call(s32[4]{0:T(128)S(1)} %and_select_fusion.part_ref, bf16[256,3072]{1,0:T(8,128)(2,1)} %collective-permute-done.3.refs_0_, bf16[256,3072]{1,0:T(8,128)(2,1)S(1)} %collective-permute-done.11.refs_1_, bf16[3,3072,128]{2,1,0:T(8,128)(2,1)S(1)} %copy-done, ...), custom_call_target="tpu_custom_call" | custom-call | flops 1 | bytes 1 | tf_op jit(solution)/shard_map/pallas_call | solution.py:84
  73.1 2.5 %collective-permute-start.15 = (bf16[3,512,128]{2,1,0:T(8,128)(2,1)}, bf16[3,512,128]{2,1,0:T(8,128)(2,1)S(1)}, u32[]{:S(2)}, u32[]{:S(2)}) collective-permute-start(bf16[3,512,128]{2,1,0:T(8,128)(2,1)} %copy-done.15), channel_id=1, source_target_pairs={{0,8},{4,12},{64,72},{68,76},{8,0},{12,4},{72,64},{76,68},{1,9},{5... | collective-permute-start | bytes 1179656 | tf_op jit(solution)/shard_map/ppermute | solution.py:33
  77.8 5.0 %shard_map.107 = (bf16[3,512,128]{2,1,0:T(8,128)(2,1)S(1)}, bf16[3,512,128]{2,1,0:T(8,128)(2,1)S(1)}) custom-call(s32[4]{0:T(128)S(1)} %and_select_fusion.part_ref, bf16[128,3072]{1,0:T(8,128)(2,1)} %collective-permute-done.7.refs_0_, bf16[128,3072]{1,0:T(8,128)(2,1)} %collective-permute-done.8.refs_1_, bf16[128,3072]{1,0:T(8,128)(2,1)} %collective-permute-done.12.refs_2_, ...), custom_call_target="tpu_custom_call" | custom-call | flops 1 | bytes 1 | tf_op jit(solution)/shard_map/pallas_call | solution.py:84
  82.9 8.4 %shard_map.108 = (f32[2560,128]{1,0:T(8,128)S(1)}, f32[2560,256]{1,0:T(8,128)S(1)}) custom-call(s32[16]{0:T(128)S(1)} %stack.67.place_ref, bf16[3,512,128]{2,1,0:T(8,128)(2,1)S(1)} %copy-done.6, bf16[3,512,128]{2,1,0:T(8,128)(2,1)S(1)} %copy-done.10, bf16[3,512,128]{2,1,0:T(8,128)(2,1)S(1)} %copy-done.12, ...), custom_call_target="tpu_custom_call" | custom-call | flops 1 | bytes 1 | tf_op jit(solution)/shard_map/pallas_call | solution.py:175
  93.0 8.5 %shard_map.109 = (f32[3584,128]{1,0:T(8,128)S(1)}, f32[3584,256]{1,0:T(8,128)S(1)}) custom-call(s32[16]{0:T(128)S(1)} %stack.67.place_ref, bf16[3,512,128]{2,1,0:T(8,128)(2,1)S(1)} %copy-done.6, bf16[3,512,128]{2,1,0:T(8,128)(2,1)S(1)} %copy-done.10, bf16[3,512,128]{2,1,0:T(8,128)(2,1)S(1)} %copy-done.12, ...), custom_call_target="tpu_custom_call" | custom-call | flops 1 | bytes 1 | tf_op jit(solution)/shard_map/pallas_call | solution.py:175
  102.6 7.8 %shard_map.110 = bf16[4096,128]{1,0:T(8,128)(2,1)} custom-call(s32[16]{0:T(128)S(1)} %stack.67.place_ref, bf16[3,512,128]{2,1,0:T(8,128)(2,1)S(1)} %copy-done.6, bf16[3,512,128]{2,1,0:T(8,128)(2,1)S(1)} %copy-done.10, bf16[3,512,128]{2,1,0:T(8,128)(2,1)S(1)} %copy-done.12, bf16[3,512,128]{2,1,0:T(8,128)(2,1)S(1)} %get-tuple-element.50.refs_3_, ...), custom_call_target="tpu_custom_call" | custom-call | flops 1 | bytes 1 | tf_op jit(solution)/shard_map/pallas_call | solution.py:175
  110.5 6.0 %all-to-all-start = ((bf16[16,256,128]{2,1,0:T(8,128)(2,1)}), bf16[16,256,128]{2,1,0:T(8,128)(2,1)S(1)}, u32[]{:S(2)}, u32[]{:S(2)}) async-start(bf16[16,256,128]{2,1,0:T(8,128)(2,1)} %bitcast.20), calls=%async_computation | async-start | bytes 2097152 | tf_op jit(solution)/shard_map/all_to_all | solution.py:391
  116.9 16.8 %all-to-all-done.att_ref = bf16[16,256,128]{2,1,0:T(8,128)(2,1)S(1)} async-done(((bf16[16,256,128]{2,1,0:T(8,128)(2,1)}), bf16[16,256,128]{2,1,0:T(8,128)(2,1)S(1)}, u32[]{:S(2)}, u32[]{:S(2)}) %all-to-all-start) | async-done | bytes 1048608 | tf_op jit(solution)/shard_map/all_to_all | solution.py:391
  135.4 4.7 %all-to-all-start.1 = ((bf16[8,128,128]{2,1,0:T(8,128)(2,1)}), bf16[8,128,128]{2,1,0:T(8,128)(2,1)S(1)}, u32[]{:S(2)}, u32[]{:S(2)}) async-start(bf16[8,128,128]{2,1,0:T(8,128)(2,1)} %shard_map.111), calls=%async_computation.1 | async-start | bytes 524288 | tf_op jit(solution)/shard_map/all_to_all | solution.py:400
  146.6 4.9 %collective-permute-start.17 = (bf16[64,128]{1,0:T(8,128)(2,1)S(1)}, bf16[64,128]{1,0:T(8,128)(2,1)S(1)}, u32[]{:S(2)}, u32[]{:S(2)}) collective-permute-start(bf16[64,128]{1,0:T(8,128)(2,1)S(1)} %get-tuple-element.67), channel_id=1, source_target_pairs={{0,4},{4,8},{8,12},{12,16},{16,20},{20,24},{24,28},{28,32},{32,36}... | collective-permute-start | bytes 49160 | tf_op jit(solution)/shard_map/ppermute | solution.py:407
  151.5 1.9 %collective-permute-start.18 = (bf16[64,128]{1,0:T(8,128)(2,1)S(1)}, bf16[64,128]{1,0:T(8,128)(2,1)S(1)}, u32[]{:S(2)}, u32[]{:S(2)}) collective-permute-start(bf16[64,128]{1,0:T(8,128)(2,1)S(1)} %get-tuple-element.66), channel_id=1, source_target_pairs={{4,0},{8,4},{12,8},{16,12},{20,16},{24,20},{28,24},{32,28},{36,32}... | collective-permute-start | bytes 49160 | tf_op jit(solution)/shard_map/ppermute | solution.py:408
  154.4 3.8 %collective-permute-done.18.after_ref = bf16[64,128]{1,0:T(8,128)(2,1)S(1)} collective-permute-done((bf16[64,128]{1,0:T(8,128)(2,1)S(1)}, bf16[64,128]{1,0:T(8,128)(2,1)S(1)}, u32[]{:S(2)}, u32[]{:S(2)}) %collective-permute-start.18) | collective-permute-done | bytes 16416 | tf_op jit(solution)/shard_map/ppermute | solution.py:408
  158.1 2.4 %shard_map.113 = bf16[512,8,128]{2,1,0:T(8,128)(2,1)} custom-call(s32[1]{0:T(128)} %dynamic_slice.20.limit_ref, f32[2,512,512]{2,1,0:T(8,128)S(1)} %shard_map.112.inner_ref, bf16[64,128]{1,0:T(8,128)(2,1)S(1)} %collective-permute-done.17.before_ref, bf16[64,128]{1,0:T(8,128)(2,1)S(1)} %collective-permute-done.18.after_ref, bf16[432,512]{1,0:T(8,128)(2,1)S(1)} %bitcast.45), custom_call_target="tpu_custom_call" | custom-call | flops 1 | bytes 1 | tf_op jit(solution)/shard_map/pallas_call | solution.py:318
  (91 shorter events, 26.8 us)
Async XLA Ops:
  5.3 21.4 %collective-permute-start.1 = (bf16[256,3072]{1,0:T(8,128)(2,1)}, bf16[256,3072]{1,0:T(8,128)(2,1)}, u32[]{:S(2)}, u32[]{:S(2)}) collective-permute-start(bf16[256,3072]{1,0:T(8,128)(2,1)} %fusion.3.refs_0_), channel_id=1, source_target_pairs={{0,4},{4,0},{64,68},{68,64},{8,12},{12,8},{72,76},{76,72},{1,5},{5... | collective-permute-start | bytes 4718600 | tf_op jit(solution)/shard_map/ppermute | solution.py:33
  6.7 37.6 %collective-permute-start.2 = (bf16[256,3072]{1,0:T(8,128)(2,1)}, bf16[256,3072]{1,0:T(8,128)(2,1)}, u32[]{:S(2)}, u32[]{:S(2)}) collective-permute-start(bf16[256,3072]{1,0:T(8,128)(2,1)} %fusion.3.refs_0_), channel_id=1, source_target_pairs={{0,16},{4,20},{64,80},{68,84},{8,24},{12,28},{72,88},{76,92},{1,17... | collective-permute-start | bytes 4718600 | tf_op jit(solution)/shard_map/ppermute | solution.py:33
  8.0 37.4 %collective-permute-start.3 = (bf16[256,3072]{1,0:T(8,128)(2,1)}, bf16[256,3072]{1,0:T(8,128)(2,1)}, u32[]{:S(2)}, u32[]{:S(2)}) collective-permute-start(bf16[256,3072]{1,0:T(8,128)(2,1)} %fusion.3.refs_0_), channel_id=1, source_target_pairs={{0,48},{4,52},{64,112},{68,116},{8,56},{12,60},{72,120},{76,124},{... | collective-permute-start | bytes 4718600 | tf_op jit(solution)/shard_map/ppermute | solution.py:33
  9.4 17.2 %collective-permute-start = (bf16[3,768,128]{2,1,0:T(8,128)(2,1)S(1)}, bf16[3,768,128]{2,1,0:T(8,128)(2,1)S(1)}, u32[]{:S(2)}, u32[]{:S(2)}) collective-permute-start(bf16[3,768,128]{2,1,0:T(8,128)(2,1)S(1)} %get-tuple-element.65), channel_id=1, source_target_pairs={{0,72},{4,76},{64,8},{68,12},{8,64},{12,68},{72,0},{76,4},{1,73},{... | collective-permute-start | bytes 1769480 | tf_op jit(solution)/shard_map/ppermute | solution.py:33
  26.6 20.0 %collective-permute-start.4 = (bf16[3,768,128]{2,1,0:T(8,128)(2,1)S(1)}, bf16[3,768,128]{2,1,0:T(8,128)(2,1)S(1)}, u32[]{:S(2)}, u32[]{:S(2)}) collective-permute-start(bf16[3,768,128]{2,1,0:T(8,128)(2,1)S(1)} %collective-permute-done.refs_3_.refs_5_), channel_id=1, source_target_pairs={{0,3},{4,7},{64,67},{68,71},{8,11},{12,15},{72,75},{76,79},{1,0},{... | collective-permute-start | bytes 1769480 | tf_op jit(solution)/shard_map/ppermute | solution.py:33
  29.4 17.2 %collective-permute-start.5 = (bf16[3,768,128]{2,1,0:T(8,128)(2,1)S(1)}, bf16[3,768,128]{2,1,0:T(8,128)(2,1)S(1)}, u32[]{:S(2)}, u32[]{:S(2)}) collective-permute-start(bf16[3,768,128]{2,1,0:T(8,128)(2,1)S(1)} %get-tuple-element.34), channel_id=1, source_target_pairs={{0,72},{4,76},{64,8},{68,12},{8,64},{12,68},{72,0},{76,4},{1,73},{... | collective-permute-start | bytes 1769480 | tf_op jit(solution)/shard_map/ppermute | solution.py:33
  31.7 14.9 %collective-permute-start.6 = (bf16[3,768,128]{2,1,0:T(8,128)(2,1)S(1)}, bf16[3,768,128]{2,1,0:T(8,128)(2,1)S(1)}, u32[]{:S(2)}, u32[]{:S(2)}) collective-permute-start(bf16[3,768,128]{2,1,0:T(8,128)(2,1)S(1)} %collective-permute-done.refs_3_.refs_5_), channel_id=1, source_target_pairs={{0,1},{4,5},{64,65},{68,69},{8,9},{12,13},{72,73},{76,77},{1,2},{5... | collective-permute-start | bytes 1769480 | tf_op jit(solution)/shard_map/ppermute | solution.py:33
  46.7 12.3 %collective-permute-start.10 = (bf16[256,3072]{1,0:T(8,128)(2,1)}, bf16[256,3072]{1,0:T(8,128)(2,1)S(1)}, u32[]{:S(2)}, u32[]{:S(2)}) collective-permute-start(bf16[256,3072]{1,0:T(8,128)(2,1)} %collective-permute-done.2.refs_0_), channel_id=1, source_target_pairs={{0,4},{4,0},{64,68},{68,64},{8,12},{12,8},{72,76},{76,72},{1,5},{5... | collective-permute-start | bytes 4718600 | tf_op jit(solution)/shard_map/ppermute | solution.py:33
  48.7 15.5 %collective-permute-start.11 = (bf16[256,3072]{1,0:T(8,128)(2,1)}, bf16[256,3072]{1,0:T(8,128)(2,1)S(1)}, u32[]{:S(2)}, u32[]{:S(2)}) collective-permute-start(bf16[256,3072]{1,0:T(8,128)(2,1)} %collective-permute-done.3.refs_0_), channel_id=1, source_target_pairs={{0,4},{4,0},{64,68},{68,64},{8,12},{12,8},{72,76},{76,72},{1,5},{5... | collective-permute-start | bytes 4718600 | tf_op jit(solution)/shard_map/ppermute | solution.py:33
  48.7 22.4 %collective-permute-start.7 = (bf16[128,3072]{1,0:T(8,128)(2,1)S(1)}, bf16[128,3072]{1,0:T(8,128)(2,1)}, u32[]{:S(2)}, u32[]{:S(2)}) collective-permute-start(bf16[128,3072]{1,0:T(8,128)(2,1)S(1)} %slice.34), channel_id=1, source_target_pairs={{0,16},{4,20},{64,80},{68,84},{8,24},{12,28},{72,88},{76,92},{1,17... | collective-permute-start | bytes 2359304 | tf_op jit(solution)/shard_map/ppermute | solution.py:33
  48.7 22.4 %collective-permute-start.8 = (bf16[128,3072]{1,0:T(8,128)(2,1)S(1)}, bf16[128,3072]{1,0:T(8,128)(2,1)}, u32[]{:S(2)}, u32[]{:S(2)}) collective-permute-start(bf16[128,3072]{1,0:T(8,128)(2,1)S(1)} %slice.35), channel_id=1, source_target_pairs={{0,48},{4,52},{64,112},{68,116},{8,56},{12,60},{72,120},{76,124},{... | collective-permute-start | bytes 2359304 | tf_op jit(solution)/shard_map/ppermute | solution.py:33
  56.3 14.0 %collective-permute-start.9 = (bf16[3,512,128]{2,1,0:T(8,128)(2,1)S(1)}, bf16[3,512,128]{2,1,0:T(8,128)(2,1)S(1)}, u32[]{:S(2)}, u32[]{:S(2)}) collective-permute-start(bf16[3,512,128]{2,1,0:T(8,128)(2,1)S(1)} %get-tuple-element.41), channel_id=1, source_target_pairs={{0,8},{4,12},{64,72},{68,76},{8,0},{12,4},{72,64},{76,68},{1,9},{5... | collective-permute-start | bytes 1179656 | tf_op jit(solution)/shard_map/ppermute | solution.py:33
  71.1 4.5 %collective-permute-start.12 = (bf16[128,3072]{1,0:T(8,128)(2,1)}, bf16[128,3072]{1,0:T(8,128)(2,1)}, u32[]{:S(2)}, u32[]{:S(2)}) collective-permute-start(bf16[128,3072]{1,0:T(8,128)(2,1)} %collective-permute-done.7.refs_0_), channel_id=1, source_target_pairs={{0,4},{4,0},{64,68},{68,64},{8,12},{12,8},{72,76},{76,72},{1,5},{5... | collective-permute-start | bytes 2359304 | tf_op jit(solution)/shard_map/ppermute | solution.py:33
  72.3 3.4 %collective-permute-start.13 = (bf16[128,3072]{1,0:T(8,128)(2,1)}, bf16[128,3072]{1,0:T(8,128)(2,1)}, u32[]{:S(2)}, u32[]{:S(2)}) collective-permute-start(bf16[128,3072]{1,0:T(8,128)(2,1)} %collective-permute-done.8.refs_1_), channel_id=1, source_target_pairs={{0,4},{4,0},{64,68},{68,64},{8,12},{12,8},{72,76},{76,72},{1,5},{5... | collective-permute-start | bytes 2359304 | tf_op jit(solution)/shard_map/ppermute | solution.py:33
  72.5 19.2 %collective-permute-start.14 = (bf16[3,512,128]{2,1,0:T(8,128)(2,1)}, bf16[3,512,128]{2,1,0:T(8,128)(2,1)S(1)}, u32[]{:S(2)}, u32[]{:S(2)}) collective-permute-start(bf16[3,512,128]{2,1,0:T(8,128)(2,1)} %copy-done.14), channel_id=1, source_target_pairs={{0,8},{4,12},{64,72},{68,76},{8,0},{12,4},{72,64},{76,68},{1,9},{5... | collective-permute-start | bytes 1179656 | tf_op jit(solution)/shard_map/ppermute | solution.py:33
  73.1 19.9 %collective-permute-start.15 = (bf16[3,512,128]{2,1,0:T(8,128)(2,1)}, bf16[3,512,128]{2,1,0:T(8,128)(2,1)S(1)}, u32[]{:S(2)}, u32[]{:S(2)}) collective-permute-start(bf16[3,512,128]{2,1,0:T(8,128)(2,1)} %copy-done.15), channel_id=1, source_target_pairs={{0,8},{4,12},{64,72},{68,76},{8,0},{12,4},{72,64},{76,68},{1,9},{5... | collective-permute-start | bytes 1179656 | tf_op jit(solution)/shard_map/ppermute | solution.py:33
  91.2 11.4 %collective-permute-start.16 = (bf16[3,512,128]{2,1,0:T(8,128)(2,1)S(1)}, bf16[3,512,128]{2,1,0:T(8,128)(2,1)S(1)}, u32[]{:S(2)}, u32[]{:S(2)}) collective-permute-start(bf16[3,512,128]{2,1,0:T(8,128)(2,1)S(1)} %get-tuple-element.57), channel_id=1, source_target_pairs={{0,8},{4,12},{64,72},{68,76},{8,0},{12,4},{72,64},{76,68},{1,9},{5... | collective-permute-start | bytes 1179656 | tf_op jit(solution)/shard_map/ppermute | solution.py:33
  110.5 29.7 %copy-start.20 = (s32[8]{0:T(128)S(1)}, s32[8]{0:T(128)}, u32[]{:S(2)}) copy-start(s32[8]{0:T(128)} %param.14) | copy-start | bytes 100
  110.5 31.6 %copy-start.19 = (f32[512]{0:T(512)S(1)}, f32[512]{0:T(512)}, u32[]{:S(2)}) copy-start(f32[512]{0:T(512)} %param.17) | copy-start | bytes 6148
  110.5 32.4 %copy-start.21 = (s32[8]{0:T(128)S(1)}, s32[8]{0:T(128)}, u32[]{:S(2)}) copy-start(s32[8]{0:T(128)} %param.15) | copy-start | bytes 100
  110.5 23.3 %all-to-all-start = ((bf16[16,256,128]{2,1,0:T(8,128)(2,1)}), bf16[16,256,128]{2,1,0:T(8,128)(2,1)S(1)}, u32[]{:S(2)}, u32[]{:S(2)}) async-start(bf16[16,256,128]{2,1,0:T(8,128)(2,1)} %bitcast.20), calls=%async_computation | async-start | bytes 2097152 | tf_op jit(solution)/shard_map/all_to_all | solution.py:391
  135.4 11.2 %all-to-all-start.1 = ((bf16[8,128,128]{2,1,0:T(8,128)(2,1)}), bf16[8,128,128]{2,1,0:T(8,128)(2,1)S(1)}, u32[]{:S(2)}, u32[]{:S(2)}) async-start(bf16[8,128,128]{2,1,0:T(8,128)(2,1)} %shard_map.111), calls=%async_computation.1 | async-start | bytes 524288 | tf_op jit(solution)/shard_map/all_to_all | solution.py:400
  146.6 7.7 %collective-permute-start.17 = (bf16[64,128]{1,0:T(8,128)(2,1)S(1)}, bf16[64,128]{1,0:T(8,128)(2,1)S(1)}, u32[]{:S(2)}, u32[]{:S(2)}) collective-permute-start(bf16[64,128]{1,0:T(8,128)(2,1)S(1)} %get-tuple-element.67), channel_id=1, source_target_pairs={{0,4},{4,8},{8,12},{12,16},{16,20},{20,24},{24,28},{28,32},{32,36}... | collective-permute-start | bytes 49160 | tf_op jit(solution)/shard_map/ppermute | solution.py:407
  151.5 6.6 %collective-permute-start.18 = (bf16[64,128]{1,0:T(8,128)(2,1)S(1)}, bf16[64,128]{1,0:T(8,128)(2,1)S(1)}, u32[]{:S(2)}, u32[]{:S(2)}) collective-permute-start(bf16[64,128]{1,0:T(8,128)(2,1)S(1)} %get-tuple-element.66), channel_id=1, source_target_pairs={{4,0},{8,4},{12,8},{16,12},{20,16},{24,20},{28,24},{32,28},{36,32}... | collective-permute-start | bytes 49160 | tf_op jit(solution)/shard_map/ppermute | solution.py:408
  (19 other events, 123.9 us)

commit v2 on v0

--- a/solution.py
+++ b/solution.py
@@ -58,8 +58,7 @@
     w_ref = refs[n_tokens]
     w_parts = refs[n_tokens + 1 : n_tokens + 5]
     own_ref, away_ref = refs[n_tokens + 5 :]
-
-    def step(c, carry):
+    for c in range(w_ref.shape[0]):
         total = None
         for k in range(4):
             depth = w_parts[k].shape[1]
@@ -68,12 +67,11 @@
             columns = jnp.concatenate([w_ref[c, pl.ds(at, depth), :], w_parts[k][c]], axis=1)
             term = jnp.dot(rows, columns, preferred_element_type=jnp.float32)
             total = term if total is None else total + term
-        total = (total * jnp.where(c == 0, QUERY_SCALE, 1.0)).astype(jnp.bfloat16)
+        if c == 0:
+            total = total * QUERY_SCALE
+        total = total.astype(jnp.bfloat16)
         own_ref[c] = total[:, :HEAD_DIM]
         away_ref[c] = total[:, HEAD_DIM:]
-        return carry
-
-    lax.fori_loop(0, w_ref.shape[0], step, 0)
 
 
 def project(parts, tokens, w_qkv, w_parts):
@@ -304,11 +302,13 @@
     from_right = moved(normed, left)
     swapped = moved(normed, other_core)
     part_0, part_2, swapped = lax.optimization_barrier((part_0, part_2, swapped))
+    part_2 = moved(part_2, mirrored_z)
     part_1 = moved(part_0, lambda x, y, z, core: (x, y - 1, z, core))
     part_3 = moved(part_0, lambda x, y, z, core: (x, y + 1, z, core))
-    part_2 = moved(part_2, mirrored_z)
-    from_left, from_right, part_1, part_2, part_3 = lax.optimization_barrier(
-        (from_left, from_right, part_1, part_2, part_3)
+    near_0 = from_left[:half]
+    near_1 = from_right[half:]
+    near_0, near_1, from_left, from_right, part_1, part_2, part_3 = lax.optimization_barrier(
+        (near_0, near_1, from_left, from_right, part_1, part_2, part_3)
     )
     w_parts = (part_0, part_1, part_2, part_3)
 
@@ -316,8 +316,8 @@
         own, away = project(parts, both, w_qkv, w_parts)
         return own, moved(away, opposite_z)
 
-    far_0 = moved(from_left[:half], right)
-    far_1 = moved(from_right[half:], left)
+    far_0 = moved(near_0, right)
+    far_1 = moved(near_1, left)
     own_0, away_0 = projected(normed, swapped)
     own_1, away_1 = projected(from_left, moved(from_left, other_core))
     own_2, away_2 = projected(from_right, moved(from_right, other_core))

time: 162 us -> 161 us (level)
  transfers between devices with their start and end apart: 21 -> 21, of which waited for: 8 -> 7; matrix products, arithmetic and copies ran while one was open for 4% -> 4% of each run, Pallas kernels for 22% -> 21%
where the time goes in v2:
time: 161 us; the launch traced here: 160 us
  waiting for transfers between devices  49.7 us (31%)
  Pallas kernels  46.5 us (29%)
  starting transfers between devices  45.3 us (28%)
  local copies, waits for them, and re-layouts  11.4 us (7%)
  other arithmetic  4.6 us (3%)
  between operations  2.95 us (2%)
    ppermute x17, waiting for transfers between devices, moved(): return lax.ppermute(array, EVERY, perm)  27.1 us
    ppermute x17, starting transfers between devices, moved(): return lax.ppermute(array, EVERY, perm)  26.5 us
    pallas_call x3, Pallas kernels, phase(): pl.pallas_call(functools.partial(phase_kernel, len(old), len(new), last),...  24.7 us
    pallas_call x4, Pallas kernels, project(): pl.pallas_call(functools.partial(project_kernel, len(tokens)), in_specs=[...  17.4 us
    all_to_all x1, waiting for transfers between devices, on_device(): lax.all_to_all(head_outputs.reshape(-1, tokens, HEAD_DIM), 'seq', split_a...  16.8 us
    all_to_all x1, starting transfers between devices, on_device(): lax.all_to_all(head_outputs.reshape(-1, tokens, HEAD_DIM), 'seq', split_a...  7.32 us
    unnamed x45, local copies, waits for them, and re-layouts  6.63 us
    ppermute x1, starting transfers between devices, on_device(): before = lax.ppermute(chosen[line:], 'seq', up)  4.93 us
  transfers between devices with their start and end apart: 21, of which 7 were waited for; matrix products, arithmetic and copies ran while one was open for 4% of the time, Pallas kernels for 21%

profile of v2, /device:TPU:1, one launch (start us, length us, event | category | flops | bytes accessed | tf_op | source)
XLA Modules:
  0.0 160.5 jit_solution(17142676256392868008)
XLA Ops:
  1.6 1.9 %fusion = f32[256]{0:T(256)S(1)} fusion(bf16[1,256,3072]{2,1,0:T(8,128)(2,1)} %param.9), kind=kLoop, calls=%fused_computation.2 | loop fusion | flops 2359040 | bytes 1573888 | tf_op jit(solution)/shard_map/reduce_sum | solution.py:297
  3.5 1.7 %fusion.3.refs_0_ = bf16[256,3072]{1,0:T(8,128)(2,1)} fusion(bf16[1,256,3072]{2,1,0:T(8,128)(2,1)S(1)} %copy-done.16, f32[3072]{0:T(1024)S(1)} %bitcast.51, f32[3072]{0:T(1024)S(1)} %bitcast.50, f32[256]{0:T(256)S(1)} %add_rsqrt_fusion), kind=kLoop, calls=%fused_computation.5 | loop fusion | flops 3932160 | bytes 3171328 | tf_op jit(solution)/shard_map/convert_element_type | solution.py:298
  9.4 3.9 %collective-permute-start = (bf16[3,768,128]{2,1,0:T(8,128)(2,1)S(1)}, bf16[3,768,128]{2,1,0:T(8,128)(2,1)S(1)}, u32[]{:S(2)}, u32[]{:S(2)}) collective-permute-start(bf16[3,768,128]{2,1,0:T(8,128)(2,1)S(1)} %get-tuple-element.65), channel_id=1, source_target_pairs={{0,72},{4,76},{64,8},{68,12},{8,64},{12,68},{72,0},{76,4},{1,73},{... | collective-permute-start | bytes 1769480 | tf_op jit(solution)/shard_map/ppermute | solution.py:33
  13.4 13.3 %collective-permute-done.refs_3_.refs_5_ = bf16[3,768,128]{2,1,0:T(8,128)(2,1)S(1)} collective-permute-done((bf16[3,768,128]{2,1,0:T(8,128)(2,1)S(1)}, bf16[3,768,128]{2,1,0:T(8,128)(2,1)S(1)}, u32[]{:S(2)}, u32[]{:S(2)}) %collective-permute-start) | collective-permute-done | bytes 589856 | tf_op jit(solution)/shard_map/ppermute | solution.py:33
  26.6 2.7 %collective-permute-start.4 = (bf16[3,768,128]{2,1,0:T(8,128)(2,1)S(1)}, bf16[3,768,128]{2,1,0:T(8,128)(2,1)S(1)}, u32[]{:S(2)}, u32[]{:S(2)}) collective-permute-start(bf16[3,768,128]{2,1,0:T(8,128)(2,1)S(1)} %collective-permute-done.refs_3_.refs_5_), channel_id=1, source_target_pairs={{0,3},{4,7},{64,67},{68,71},{8,11},{12,15},{72,75},{76,79},{1,0},{... | collective-permute-start | bytes 1769480 | tf_op jit(solution)/shard_map/ppermute | solution.py:33
  29.4 2.4 %collective-permute-start.5 = (bf16[3,768,128]{2,1,0:T(8,128)(2,1)S(1)}, bf16[3,768,128]{2,1,0:T(8,128)(2,1)S(1)}, u32[]{:S(2)}, u32[]{:S(2)}) collective-permute-start(bf16[3,768,128]{2,1,0:T(8,128)(2,1)S(1)} %get-tuple-element.34), channel_id=1, source_target_pairs={{0,72},{4,76},{64,8},{68,12},{8,64},{12,68},{72,0},{76,4},{1,73},{... | collective-permute-start | bytes 1769480 | tf_op jit(solution)/shard_map/ppermute | solution.py:33
  31.7 12.5 %collective-permute-done.2.refs_0_ = bf16[256,3072]{1,0:T(8,128)(2,1)} collective-permute-done((bf16[256,3072]{1,0:T(8,128)(2,1)}, bf16[256,3072]{1,0:T(8,128)(2,1)}, u32[]{:S(2)}, u32[]{:S(2)}) %collective-permute-start.2) | collective-permute-done | bytes 1572896 | tf_op jit(solution)/shard_map/ppermute | solution.py:33
  46.7 2.0 %collective-permute-start.10 = (bf16[256,3072]{1,0:T(8,128)(2,1)}, bf16[256,3072]{1,0:T(8,128)(2,1)S(1)}, u32[]{:S(2)}, u32[]{:S(2)}) collective-permute-start(bf16[256,3072]{1,0:T(8,128)(2,1)} %collective-permute-done.2.refs_0_), channel_id=1, source_target_pairs={{0,4},{4,0},{64,68},{68,64},{8,12},{12,8},{72,76},{76,72},{1,5},{5... | collective-permute-start | bytes 4718600 | tf_op jit(solution)/shard_map/ppermute | solution.py:33
  48.7 2.7 %collective-permute-start.8 = (bf16[128,3072]{1,0:T(8,128)(2,1)S(1)}, bf16[128,3072]{1,0:T(8,128)(2,1)}, u32[]{:S(2)}, u32[]{:S(2)}) collective-permute-start(bf16[128,3072]{1,0:T(8,128)(2,1)S(1)} %slice.35), channel_id=1, source_target_pairs={{0,48},{4,52},{64,112},{68,116},{8,56},{12,60},{72,120},{76,124},{... | collective-permute-start | bytes 2359304 | tf_op jit(solution)/shard_map/ppermute | solution.py:33
  51.4 4.5 %shard_map.104 = (bf16[3,512,128]{2,1,0:T(8,128)(2,1)S(1)}, bf16[3,512,128]{2,1,0:T(8,128)(2,1)S(1)}) custom-call(s32[4]{0:T(128)S(1)} %and_select_fusion.part_ref, bf16[256,3072]{1,0:T(8,128)(2,1)} %fusion.3.refs_0_, bf16[256,3072]{1,0:T(8,128)(2,1)} %collective-permute-done.1.refs_1_, bf16[3,3072,128]{2,1,0:T(8,128)(2,1)S(1)} %copy-done, ...), custom_call_target="tpu_custom_call" | custom-call | flops 1 | bytes 1 | tf_op jit(solution)/shard_map/pallas_call | solution.py:82
  55.9 2.7 %collective-permute-start.9 = (bf16[3,512,128]{2,1,0:T(8,128)(2,1)S(1)}, bf16[3,512,128]{2,1,0:T(8,128)(2,1)S(1)}, u32[]{:S(2)}, u32[]{:S(2)}) collective-permute-start(bf16[3,512,128]{2,1,0:T(8,128)(2,1)S(1)} %get-tuple-element.41), channel_id=1, source_target_pairs={{0,8},{4,12},{64,72},{68,76},{8,0},{12,4},{72,64},{76,68},{1,9},{5... | collective-permute-start | bytes 1179656 | tf_op jit(solution)/shard_map/ppermute | solution.py:33
  58.6 4.0 %shard_map.105 = (bf16[3,512,128]{2,1,0:T(8,128)(2,1)S(1)}, bf16[3,512,128]{2,1,0:T(8,128)(2,1)S(1)}) custom-call(s32[4]{0:T(128)S(1)} %and_select_fusion.part_ref, bf16[256,3072]{1,0:T(8,128)(2,1)} %collective-permute-done.2.refs_0_, bf16[256,3072]{1,0:T(8,128)(2,1)S(1)} %collective-permute-done.10.refs_1_, bf16[3,3072,128]{2,1,0:T(8,128)(2,1)S(1)} %copy-done, ...), custom_call_target="tpu_custom_call" | custom-call | flops 1 | bytes 1 | tf_op jit(solution)/shard_map/pallas_call | solution.py:82
  63.5 4.2 %shard_map.106 = (bf16[3,512,128]{2,1,0:T(8,128)(2,1)S(1)}, bf16[3,512,128]{2,1,0:T(8,128)(2,1)S(1)}) custom-call(s32[4]{0:T(128)S(1)} %and_select_fusion.part_ref, bf16[256,3072]{1,0:T(8,128)(2,1)} %collective-permute-done.3.refs_0_, bf16[256,3072]{1,0:T(8,128)(2,1)S(1)} %collective-permute-done.11.refs_1_, bf16[3,3072,128]{2,1,0:T(8,128)(2,1)S(1)} %copy-done, ...), custom_call_target="tpu_custom_call" | custom-call | flops 1 | bytes 1 | tf_op jit(solution)/shard_map/pallas_call | solution.py:82
  76.8 4.6 %shard_map.107 = (bf16[3,512,128]{2,1,0:T(8,128)(2,1)S(1)}, bf16[3,512,128]{2,1,0:T(8,128)(2,1)S(1)}) custom-call(s32[4]{0:T(128)S(1)} %and_select_fusion.part_ref, bf16[128,3072]{1,0:T(8,128)(2,1)} %collective-permute-done.7.refs_0_, bf16[128,3072]{1,0:T(8,128)(2,1)} %collective-permute-done.8.refs_1_, bf16[128,3072]{1,0:T(8,128)(2,1)} %collective-permute-done.12.refs_2_, ...), custom_call_target="tpu_custom_call" | custom-call | flops 1 | bytes 1 | tf_op jit(solution)/shard_map/pallas_call | solution.py:82
  81.4 8.4 %shard_map.108 = (f32[2560,128]{1,0:T(8,128)S(1)}, f32[2560,256]{1,0:T(8,128)S(1)}) custom-call(s32[16]{0:T(128)S(1)} %stack.67.place_ref, bf16[3,512,128]{2,1,0:T(8,128)(2,1)S(1)} %copy-done.6, bf16[3,512,128]{2,1,0:T(8,128)(2,1)S(1)} %copy-done.10, bf16[3,512,128]{2,1,0:T(8,128)(2,1)S(1)} %copy-done.12, ...), custom_call_target="tpu_custom_call" | custom-call | flops 1 | bytes 1 | tf_op jit(solution)/shard_map/pallas_call | solution.py:173
  92.1 8.5 %shard_map.109 = (f32[3584,128]{1,0:T(8,128)S(1)}, f32[3584,256]{1,0:T(8,128)S(1)}) custom-call(s32[16]{0:T(128)S(1)} %stack.67.place_ref, bf16[3,512,128]{2,1,0:T(8,128)(2,1)S(1)} %copy-done.6, bf16[3,512,128]{2,1,0:T(8,128)(2,1)S(1)} %copy-done.10, bf16[3,512,128]{2,1,0:T(8,128)(2,1)S(1)} %copy-done.12, ...), custom_call_target="tpu_custom_call" | custom-call | flops 1 | bytes 1 | tf_op jit(solution)/shard_map/pallas_call | solution.py:173
  101.0 7.8 %shard_map.110 = bf16[4096,128]{1,0:T(8,128)(2,1)} custom-call(s32[16]{0:T(128)S(1)} %stack.67.place_ref, bf16[3,512,128]{2,1,0:T(8,128)(2,1)S(1)} %copy-done.6, bf16[3,512,128]{2,1,0:T(8,128)(2,1)S(1)} %copy-done.10, bf16[3,512,128]{2,1,0:T(8,128)(2,1)S(1)} %copy-done.12, bf16[3,512,128]{2,1,0:T(8,128)(2,1)S(1)} %get-tuple-element.50.refs_3_, ...), custom_call_target="tpu_custom_call" | custom-call | flops 1 | bytes 1 | tf_op jit(solution)/shard_map/pallas_call | solution.py:173
  108.8 7.3 %all-to-all-start = ((bf16[16,256,128]{2,1,0:T(8,128)(2,1)}), bf16[16,256,128]{2,1,0:T(8,128)(2,1)S(1)}, u32[]{:S(2)}, u32[]{:S(2)}) async-start(bf16[16,256,128]{2,1,0:T(8,128)(2,1)} %bitcast.20), calls=%async_computation | async-start | bytes 2097152 | tf_op jit(solution)/shard_map/all_to_all | solution.py:343
  116.5 16.8 %all-to-all-done.att_ref = bf16[16,256,128]{2,1,0:T(8,128)(2,1)S(1)} async-done(((bf16[16,256,128]{2,1,0:T(8,128)(2,1)}), bf16[16,256,128]{2,1,0:T(8,128)(2,1)S(1)}, u32[]{:S(2)}, u32[]{:S(2)}) %all-to-all-start) | async-done | bytes 1048608 | tf_op jit(solution)/shard_map/all_to_all | solution.py:343
  135.1 4.7 %all-to-all-start.1 = ((bf16[8,128,128]{2,1,0:T(8,128)(2,1)}), bf16[8,128,128]{2,1,0:T(8,128)(2,1)S(1)}, u32[]{:S(2)}, u32[]{:S(2)}) async-start(bf16[8,128,128]{2,1,0:T(8,128)(2,1)} %shard_map.111), calls=%async_computation.1 | async-start | bytes 524288 | tf_op jit(solution)/shard_map/all_to_all | solution.py:352
  146.2 4.9 %collective-permute-start.17 = (bf16[64,128]{1,0:T(8,128)(2,1)S(1)}, bf16[64,128]{1,0:T(8,128)(2,1)S(1)}, u32[]{:S(2)}, u32[]{:S(2)}) collective-permute-start(bf16[64,128]{1,0:T(8,128)(2,1)S(1)} %get-tuple-element.67), channel_id=1, source_target_pairs={{0,4},{4,8},{8,12},{12,16},{16,20},{20,24},{24,28},{28,32},{32,36}... | collective-permute-start | bytes 49160 | tf_op jit(solution)/shard_map/ppermute | solution.py:359
  151.2 1.9 %collective-permute-start.18 = (bf16[64,128]{1,0:T(8,128)(2,1)S(1)}, bf16[64,128]{1,0:T(8,128)(2,1)S(1)}, u32[]{:S(2)}, u32[]{:S(2)}) collective-permute-start(bf16[64,128]{1,0:T(8,128)(2,1)S(1)} %get-tuple-element.66), channel_id=1, source_target_pairs={{4,0},{8,4},{12,8},{16,12},{20,16},{24,20},{28,24},{32,28},{36,32}... | collective-permute-start | bytes 49160 | tf_op jit(solution)/shard_map/ppermute | solution.py:360
  153.1 4.6 %collective-permute-done.18.after_ref = bf16[64,128]{1,0:T(8,128)(2,1)S(1)} collective-permute-done((bf16[64,128]{1,0:T(8,128)(2,1)S(1)}, bf16[64,128]{1,0:T(8,128)(2,1)S(1)}, u32[]{:S(2)}, u32[]{:S(2)}) %collective-permute-start.18) | collective-permute-done | bytes 16416 | tf_op jit(solution)/shard_map/ppermute | solution.py:360
  157.7 2.7 %shard_map.112 = bf16[512,8,128]{2,1,0:T(8,128)(2,1)} custom-call(s32[1]{0:T(128)} %dynamic_slice.20.limit_ref, bf16[128,128]{1,0:T(8,128)(2,1)S(1)} %dynamic-slice_bitcast_fusion.rows_ref, bf16[64,128]{1,0:T(8,128)(2,1)S(1)} %collective-permute-done.17.before_ref, bf16[64,128]{1,0:T(8,128)(2,1)S(1)} %collective-permute-done.18.after_ref, ...), custom_call_target="tpu_custom_call" | custom-call | flops 1 | bytes 1 | tf_op jit(solution)/shard_map/pallas_call | solution.py:270
  (90 shorter events, 26.6 us)
Async XLA Ops:
  5.3 21.4 %collective-permute-start.1 = (bf16[256,3072]{1,0:T(8,128)(2,1)}, bf16[256,3072]{1,0:T(8,128)(2,1)}, u32[]{:S(2)}, u32[]{:S(2)}) collective-permute-start(bf16[256,3072]{1,0:T(8,128)(2,1)} %fusion.3.refs_0_), channel_id=1, source_target_pairs={{0,4},{4,0},{64,68},{68,64},{8,12},{12,8},{72,76},{76,72},{1,5},{5... | collective-permute-start | bytes 4718600 | tf_op jit(solution)/shard_map/ppermute | solution.py:33
  6.7 37.6 %collective-permute-start.2 = (bf16[256,3072]{1,0:T(8,128)(2,1)}, bf16[256,3072]{1,0:T(8,128)(2,1)}, u32[]{:S(2)}, u32[]{:S(2)}) collective-permute-start(bf16[256,3072]{1,0:T(8,128)(2,1)} %fusion.3.refs_0_), channel_id=1, source_target_pairs={{0,16},{4,20},{64,80},{68,84},{8,24},{12,28},{72,88},{76,92},{1,17... | collective-permute-start | bytes 4718600 | tf_op jit(solution)/shard_map/ppermute | solution.py:33
  8.0 37.4 %collective-permute-start.3 = (bf16[256,3072]{1,0:T(8,128)(2,1)}, bf16[256,3072]{1,0:T(8,128)(2,1)}, u32[]{:S(2)}, u32[]{:S(2)}) collective-permute-start(bf16[256,3072]{1,0:T(8,128)(2,1)} %fusion.3.refs_0_), channel_id=1, source_target_pairs={{0,48},{4,52},{64,112},{68,116},{8,56},{12,60},{72,120},{76,124},{... | collective-permute-start | bytes 4718600 | tf_op jit(solution)/shard_map/ppermute | solution.py:33
  9.4 17.2 %collective-permute-start = (bf16[3,768,128]{2,1,0:T(8,128)(2,1)S(1)}, bf16[3,768,128]{2,1,0:T(8,128)(2,1)S(1)}, u32[]{:S(2)}, u32[]{:S(2)}) collective-permute-start(bf16[3,768,128]{2,1,0:T(8,128)(2,1)S(1)} %get-tuple-element.65), channel_id=1, source_target_pairs={{0,72},{4,76},{64,8},{68,12},{8,64},{12,68},{72,0},{76,4},{1,73},{... | collective-permute-start | bytes 1769480 | tf_op jit(solution)/shard_map/ppermute | solution.py:33
  26.6 20.0 %collective-permute-start.4 = (bf16[3,768,128]{2,1,0:T(8,128)(2,1)S(1)}, bf16[3,768,128]{2,1,0:T(8,128)(2,1)S(1)}, u32[]{:S(2)}, u32[]{:S(2)}) collective-permute-start(bf16[3,768,128]{2,1,0:T(8,128)(2,1)S(1)} %collective-permute-done.refs_3_.refs_5_), channel_id=1, source_target_pairs={{0,3},{4,7},{64,67},{68,71},{8,11},{12,15},{72,75},{76,79},{1,0},{... | collective-permute-start | bytes 1769480 | tf_op jit(solution)/shard_map/ppermute | solution.py:33
  29.4 17.2 %collective-permute-start.5 = (bf16[3,768,128]{2,1,0:T(8,128)(2,1)S(1)}, bf16[3,768,128]{2,1,0:T(8,128)(2,1)S(1)}, u32[]{:S(2)}, u32[]{:S(2)}) collective-permute-start(bf16[3,768,128]{2,1,0:T(8,128)(2,1)S(1)} %get-tuple-element.34), channel_id=1, source_target_pairs={{0,72},{4,76},{64,8},{68,12},{8,64},{12,68},{72,0},{76,4},{1,73},{... | collective-permute-start | bytes 1769480 | tf_op jit(solution)/shard_map/ppermute | solution.py:33
  31.7 14.9 %collective-permute-start.6 = (bf16[3,768,128]{2,1,0:T(8,128)(2,1)S(1)}, bf16[3,768,128]{2,1,0:T(8,128)(2,1)S(1)}, u32[]{:S(2)}, u32[]{:S(2)}) collective-permute-start(bf16[3,768,128]{2,1,0:T(8,128)(2,1)S(1)} %collective-permute-done.refs_3_.refs_5_), channel_id=1, source_target_pairs={{0,1},{4,5},{64,65},{68,69},{8,9},{12,13},{72,73},{76,77},{1,2},{5... | collective-permute-start | bytes 1769480 | tf_op jit(solution)/shard_map/ppermute | solution.py:33
  46.7 11.9 %collective-permute-start.10 = (bf16[256,3072]{1,0:T(8,128)(2,1)}, bf16[256,3072]{1,0:T(8,128)(2,1)S(1)}, u32[]{:S(2)}, u32[]{:S(2)}) collective-permute-start(bf16[256,3072]{1,0:T(8,128)(2,1)} %collective-permute-done.2.refs_0_), channel_id=1, source_target_pairs={{0,4},{4,0},{64,68},{68,64},{8,12},{12,8},{72,76},{76,72},{1,5},{5... | collective-permute-start | bytes 4718600 | tf_op jit(solution)/shard_map/ppermute | solution.py:33
  48.7 14.8 %collective-permute-start.11 = (bf16[256,3072]{1,0:T(8,128)(2,1)}, bf16[256,3072]{1,0:T(8,128)(2,1)S(1)}, u32[]{:S(2)}, u32[]{:S(2)}) collective-permute-start(bf16[256,3072]{1,0:T(8,128)(2,1)} %collective-permute-done.3.refs_0_), channel_id=1, source_target_pairs={{0,4},{4,0},{64,68},{68,64},{8,12},{12,8},{72,76},{76,72},{1,5},{5... | collective-permute-start | bytes 4718600 | tf_op jit(solution)/shard_map/ppermute | solution.py:33
  48.7 21.2 %collective-permute-start.7 = (bf16[128,3072]{1,0:T(8,128)(2,1)S(1)}, bf16[128,3072]{1,0:T(8,128)(2,1)}, u32[]{:S(2)}, u32[]{:S(2)}) collective-permute-start(bf16[128,3072]{1,0:T(8,128)(2,1)S(1)} %slice.34), channel_id=1, source_target_pairs={{0,16},{4,20},{64,80},{68,84},{8,24},{12,28},{72,88},{76,92},{1,17... | collective-permute-start | bytes 2359304 | tf_op jit(solution)/shard_map/ppermute | solution.py:33
  48.7 21.2 %collective-permute-start.8 = (bf16[128,3072]{1,0:T(8,128)(2,1)S(1)}, bf16[128,3072]{1,0:T(8,128)(2,1)}, u32[]{:S(2)}, u32[]{:S(2)}) collective-permute-start(bf16[128,3072]{1,0:T(8,128)(2,1)S(1)} %slice.35), channel_id=1, source_target_pairs={{0,48},{4,52},{64,112},{68,116},{8,56},{12,60},{72,120},{76,124},{... | collective-permute-start | bytes 2359304 | tf_op jit(solution)/shard_map/ppermute | solution.py:33
  55.9 13.3 %collective-permute-start.9 = (bf16[3,512,128]{2,1,0:T(8,128)(2,1)S(1)}, bf16[3,512,128]{2,1,0:T(8,128)(2,1)S(1)}, u32[]{:S(2)}, u32[]{:S(2)}) collective-permute-start(bf16[3,512,128]{2,1,0:T(8,128)(2,1)S(1)} %get-tuple-element.41), channel_id=1, source_target_pairs={{0,8},{4,12},{64,72},{68,76},{8,0},{12,4},{72,64},{76,68},{1,9},{5... | collective-permute-start | bytes 1179656 | tf_op jit(solution)/shard_map/ppermute | solution.py:33
  70.0 4.7 %collective-permute-start.12 = (bf16[128,3072]{1,0:T(8,128)(2,1)}, bf16[128,3072]{1,0:T(8,128)(2,1)}, u32[]{:S(2)}, u32[]{:S(2)}) collective-permute-start(bf16[128,3072]{1,0:T(8,128)(2,1)} %collective-permute-done.7.refs_0_), channel_id=1, source_target_pairs={{0,4},{4,0},{64,68},{68,64},{8,12},{12,8},{72,76},{76,72},{1,5},{5... | collective-permute-start | bytes 2359304 | tf_op jit(solution)/shard_map/ppermute | solution.py:33
  71.2 3.4 %collective-permute-start.13 = (bf16[128,3072]{1,0:T(8,128)(2,1)}, bf16[128,3072]{1,0:T(8,128)(2,1)}, u32[]{:S(2)}, u32[]{:S(2)}) collective-permute-start(bf16[128,3072]{1,0:T(8,128)(2,1)} %collective-permute-done.8.refs_1_), channel_id=1, source_target_pairs={{0,4},{4,0},{64,68},{68,64},{8,12},{12,8},{72,76},{76,72},{1,5},{5... | collective-permute-start | bytes 2359304 | tf_op jit(solution)/shard_map/ppermute | solution.py:33
  71.4 19.8 %collective-permute-start.14 = (bf16[3,512,128]{2,1,0:T(8,128)(2,1)}, bf16[3,512,128]{2,1,0:T(8,128)(2,1)S(1)}, u32[]{:S(2)}, u32[]{:S(2)}) collective-permute-start(bf16[3,512,128]{2,1,0:T(8,128)(2,1)} %copy-done.14), channel_id=1, source_target_pairs={{0,8},{4,12},{64,72},{68,76},{8,0},{12,4},{72,64},{76,68},{1,9},{5... | collective-permute-start | bytes 1179656 | tf_op jit(solution)/shard_map/ppermute | solution.py:33
  72.9 19.1 %collective-permute-start.15 = (bf16[3,512,128]{2,1,0:T(8,128)(2,1)}, bf16[3,512,128]{2,1,0:T(8,128)(2,1)S(1)}, u32[]{:S(2)}, u32[]{:S(2)}) collective-permute-start(bf16[3,512,128]{2,1,0:T(8,128)(2,1)} %copy-done.15), channel_id=1, source_target_pairs={{0,8},{4,12},{64,72},{68,76},{8,0},{12,4},{72,64},{76,68},{1,9},{5... | collective-permute-start | bytes 1179656 | tf_op jit(solution)/shard_map/ppermute | solution.py:33
  89.8 11.2 %collective-permute-start.16 = (bf16[3,512,128]{2,1,0:T(8,128)(2,1)S(1)}, bf16[3,512,128]{2,1,0:T(8,128)(2,1)S(1)}, u32[]{:S(2)}, u32[]{:S(2)}) collective-permute-start(bf16[3,512,128]{2,1,0:T(8,128)(2,1)S(1)} %get-tuple-element.57), channel_id=1, source_target_pairs={{0,8},{4,12},{64,72},{68,76},{8,0},{12,4},{72,64},{76,68},{1,9},{5... | collective-permute-start | bytes 1179656 | tf_op jit(solution)/shard_map/ppermute | solution.py:33
  108.8 30.9 %copy-start.20 = (s32[8]{0:T(128)S(1)}, s32[8]{0:T(128)}, u32[]{:S(2)}) copy-start(s32[8]{0:T(128)} %param.14) | copy-start | bytes 100
  108.8 32.8 %copy-start.19 = (f32[512]{0:T(512)S(1)}, f32[512]{0:T(512)}, u32[]{:S(2)}) copy-start(f32[512]{0:T(512)} %param.17) | copy-start | bytes 6148
  108.8 33.6 %copy-start.21 = (s32[8]{0:T(128)S(1)}, s32[8]{0:T(128)}, u32[]{:S(2)}) copy-start(s32[8]{0:T(128)} %param.15) | copy-start | bytes 100
  108.8 24.5 %all-to-all-start = ((bf16[16,256,128]{2,1,0:T(8,128)(2,1)}), bf16[16,256,128]{2,1,0:T(8,128)(2,1)S(1)}, u32[]{:S(2)}, u32[]{:S(2)}) async-start(bf16[16,256,128]{2,1,0:T(8,128)(2,1)} %bitcast.20), calls=%async_computation | async-start | bytes 2097152 | tf_op jit(solution)/shard_map/all_to_all | solution.py:343
  135.1 11.1 %all-to-all-start.1 = ((bf16[8,128,128]{2,1,0:T(8,128)(2,1)}), bf16[8,128,128]{2,1,0:T(8,128)(2,1)S(1)}, u32[]{:S(2)}, u32[]{:S(2)}) async-start(bf16[8,128,128]{2,1,0:T(8,128)(2,1)} %shard_map.111), calls=%async_computation.1 | async-start | bytes 524288 | tf_op jit(solution)/shard_map/all_to_all | solution.py:352
  146.2 6.9 %collective-permute-start.17 = (bf16[64,128]{1,0:T(8,128)(2,1)S(1)}, bf16[64,128]{1,0:T(8,128)(2,1)S(1)}, u32[]{:S(2)}, u32[]{:S(2)}) collective-permute-start(bf16[64,128]{1,0:T(8,128)(2,1)S(1)} %get-tuple-element.67), channel_id=1, source_target_pairs={{0,4},{4,8},{8,12},{12,16},{16,20},{20,24},{24,28},{28,32},{32,36}... | collective-permute-start | bytes 49160 | tf_op jit(solution)/shard_map/ppermute | solution.py:359
  151.2 6.6 %collective-permute-start.18 = (bf16[64,128]{1,0:T(8,128)(2,1)S(1)}, bf16[64,128]{1,0:T(8,128)(2,1)S(1)}, u32[]{:S(2)}, u32[]{:S(2)}) collective-permute-start(bf16[64,128]{1,0:T(8,128)(2,1)S(1)} %get-tuple-element.66), channel_id=1, source_target_pairs={{4,0},{8,4},{12,8},{16,12},{20,16},{24,20},{28,24},{32,28},{36,32}... | collective-permute-start | bytes 49160 | tf_op jit(solution)/shard_map/ppermute | solution.py:360
  (19 other events, 127.4 us)
